TPU v7x, 32 devices: a whole 2x2x4 slice. The times are simulated.
32 devices in a mesh: dp: 8 (over z, y), tensor: 4 (over x, core).
Axes of the slice: x: 2, y: 2, z: 4, core: 2. Of those that a mesh axis runs over, the one named last changes fastest.
Arguments:
- tokens: float32 [16384, 768], P(('dp', 'tensor')), may hold values from -6 to 6
- seq_ids: int32 [16384], P('dp'), may hold values from 0 to 8, as said below
- gain_attn: float32 [768], replicated, may hold values from 0.5 to 1.5
- gain_mlp: float32 [768], replicated, may hold values from 0.5 to 1.5
- w_qkv: bfloat16 [3, 768, 768], P(None, None, 'tensor'), may hold values from -0.21875 to 0.21875
- w_out: bfloat16 [768, 768], P('tensor'), may hold values from -1.25 to 1.25
- w_gu: bfloat16 [2, 768, 1152], P(None, None, 'tensor'), may hold values from -0.21875 to 0.21875
- w_down: bfloat16 [1152, 768], P('tensor'), may hold values from -0.1875 to 0.1875
- cotangent: float32 [16384, 768], P(('dp', 'tensor')), may hold values from -6 to 6
Outputs:
- output: float32 [16384, 768], P(('dp', 'tensor'))
- input_grad: float32 [16384, 768], P(('dp', 'tensor'))
- gain_attn_grad: float32 [768], replicated
- gain_mlp_grad: float32 [768], replicated
- w_qkv_grad: float32 [3, 768, 768], P(None, None, 'tensor')
- w_out_grad: float32 [768, 768], P('tensor')
- w_gu_grad: float32 [2, 768, 1152], P(None, None, 'tensor')
- w_down_grad: float32 [1152, 768], P('tensor')
Inputs may be any that keep to these rules, and one draw needn't show every extreme that they name: `seq_ids`: within each aligned block of 2048 tokens (those of one index of dp) the ids start at 0, never fall and rise by one at each new sequence; every sequence has 128 to 1024 tokens except a block's last one, which may be shorter; in every block some sequence has exactly 1024 tokens.
All inputs are finite; a program needn't handle non-finite values.
Results may differ from a plain program's by a relative error of at most 0.019.
Values may be sent and summed in bfloat16 or wider, within the bound.
A program may use at most 128 MiB of HBM per device.

v0:
```python
import jax
import jax.numpy as jnp
from jax import lax
from jax.sharding import PartitionSpec as P

HEAD_DIM = 64


EPSILON = 1e-05
ROPE_BASE = 160000.0
NEG_FILL = -1e30
INV_ROOT_TWO = 0.7071067811865476
INV_ROOT_TWO_PI = 0.3989422804014327


def norm_rows(values, gain_vec):
    center = values - jnp.mean(values, axis=-1, keepdims=True)
    spread = jnp.mean(center * center, axis=-1, keepdims=True)
    inverse = lax.rsqrt(spread + EPSILON)
    unit_rows = center * inverse
    return (unit_rows * gain_vec, unit_rows, inverse)


def norm_back(grad_rows, unit_rows, inverse, gain_vec):
    scaled = grad_rows * gain_vec
    inner = (
        scaled
        - jnp.mean(scaled, axis=-1, keepdims=True)
        - unit_rows * jnp.mean(scaled * unit_rows, axis=-1, keepdims=True)
    )
    return (inner * inverse, jnp.sum(grad_rows * unit_rows, axis=0))


def positions_of(seq_rows):
    length = seq_rows.shape[0]
    steps_all = jnp.arange(length, dtype=jnp.int32)
    before = jnp.concatenate([seq_rows[:1] - 1, seq_rows[:-1]], axis=0)
    change_marks = jnp.where(seq_rows != before, steps_all, 0)
    return (steps_all - lax.cummax(change_marks, axis=0)).astype(jnp.float32)


def rotary_tables(places, width):
    half_width = width // 2
    frequency = ROPE_BASE ** (-(jnp.arange(half_width, dtype=jnp.float32) * 2.0) / width)
    angles = places[:, None] * frequency[None, :]
    cosine_tab = jnp.cos(angles)
    sine_tab = jnp.sin(angles)
    return (
        jnp.concatenate([cosine_tab, cosine_tab], axis=-1),
        jnp.concatenate([sine_tab, sine_tab], axis=-1),
    )


def rotate(values, cosine_tab, sine_tab):
    half_width = values.shape[-1] // 2
    turned = jnp.concatenate([-values[..., half_width:], values[..., :half_width]], axis=-1)
    return values * cosine_tab[:, None, :] + turned * sine_tab[:, None, :]


def rotate_back(grads_in, cosine_tab, sine_tab):
    half_width = grads_in.shape[-1] // 2
    shifted = grads_in * sine_tab[:, None, :]
    turned = jnp.concatenate([shifted[..., half_width:], -shifted[..., :half_width]], axis=-1)
    return grads_in * cosine_tab[:, None, :] + turned


def gelu_parts(before_act):
    normal_cdf = 0.5 * (1.0 + lax.erf(before_act * INV_ROOT_TWO))
    density = jnp.exp(-0.5 * before_act * before_act) * INV_ROOT_TWO_PI
    return (before_act * normal_cdf, normal_cdf + before_act * density)


def shards(tokens, seq_ids, gain_attn, gain_mlp, w_qkv, w_out, w_gu, w_down, cotangent):
    group_rows = seq_ids.shape[0]
    local_width = w_out.shape[0]
    local_heads = local_width // HEAD_DIM
    scale_factor = HEAD_DIM ** (-0.5)
    block_rows = min(512, group_rows)
    blocks = group_rows // block_rows
    normed_one, unit_one, inverse_one = norm_rows(tokens, gain_attn)
    normed_all = lax.all_gather(normed_one.astype(jnp.bfloat16), "tensor", axis=0, tiled=True)
    projected = jnp.einsum("td,cde->cte", normed_all, w_qkv, preferred_element_type=jnp.float32)
    places = positions_of(seq_ids)
    cosine_tab, sine_tab = rotary_tables(places, HEAD_DIM)
    shaped = projected.reshape(3, group_rows, local_heads, HEAD_DIM)
    queries = rotate(shaped[0], cosine_tab, sine_tab).astype(jnp.bfloat16)
    key_rows = rotate(shaped[1], cosine_tab, sine_tab).astype(jnp.bfloat16)
    value_rows = shaped[2].astype(jnp.bfloat16)
    query_blocks = queries.reshape(blocks, block_rows, local_heads, HEAD_DIM)
    id_blocks = seq_ids.reshape(blocks, block_rows)

    def block_scores(query_blk, ids_blk):
        scores = (
            jnp.einsum("qhd,khd->hqk", query_blk, key_rows, preferred_element_type=jnp.float32)
            * scale_factor
        )
        same_seq = ids_blk[:, None] == seq_ids[None, :]
        return (scores, same_seq[None, :, :])

    def forward_block(block_item):
        query_blk, ids_blk = block_item
        scores, same_seq = block_scores(query_blk, ids_blk)
        scores = jnp.where(same_seq, scores, NEG_FILL)
        row_max = jnp.max(scores, axis=-1, keepdims=True)
        exponent = jnp.exp(scores - row_max)
        totals = jnp.sum(exponent, axis=-1, keepdims=True)
        weights = (exponent / totals).astype(jnp.bfloat16)
        mixed = jnp.einsum("hqk,khd->qhd", weights, value_rows, preferred_element_type=jnp.float32)
        return (mixed, row_max[..., 0] + jnp.log(totals[..., 0]))

    attended, log_totals = lax.map(forward_block, (query_blocks, id_blocks))
    attended = attended.reshape(group_rows, local_width).astype(jnp.bfloat16)
    piece = attended
    branch_one = lax.psum_scatter(
        jnp.dot(piece, w_out, preferred_element_type=jnp.float32).astype(jnp.bfloat16),
        "tensor",
        scatter_dimension=0,
        tiled=True,
    ).astype(jnp.float32)
    hidden_in = tokens + branch_one
    normed_two, unit_two, inverse_two = norm_rows(hidden_in, gain_mlp)
    normed_two_all = lax.all_gather(normed_two.astype(jnp.bfloat16), "tensor", axis=0, tiled=True)
    gate_up = jnp.einsum("td,cdf->ctf", normed_two_all, w_gu, preferred_element_type=jnp.float32)
    gelu_value, gelu_slope = gelu_parts(gate_up[0])
    activated = (gelu_value * gate_up[1]).astype(jnp.bfloat16)
    piece = activated
    branch_two = lax.psum_scatter(
        jnp.dot(piece, w_down, preferred_element_type=jnp.float32).astype(jnp.bfloat16),
        "tensor",
        scatter_dimension=0,
        tiled=True,
    ).astype(jnp.float32)
    output = hidden_in + branch_two
    grad_two_all = lax.all_gather(cotangent.astype(jnp.bfloat16), "tensor", axis=0, tiled=True)
    grad_down = jnp.einsum("tf,td->fd", activated, grad_two_all, preferred_element_type=jnp.float32)
    grad_act = jnp.einsum("td,fd->tf", grad_two_all, w_down, preferred_element_type=jnp.float32)
    grad_gate_up = jnp.stack([grad_act * gate_up[1] * gelu_slope, grad_act * gelu_value]).astype(
        jnp.bfloat16
    )
    grad_gu = jnp.einsum(
        "td,ctf->cdf", normed_two_all, grad_gate_up, preferred_element_type=jnp.float32
    )
    piece = grad_gate_up
    grad_normed_two = lax.psum_scatter(
        jnp.einsum("ctf,cdf->td", piece, w_gu, preferred_element_type=jnp.float32).astype(
            jnp.bfloat16
        ),
        "tensor",
        scatter_dimension=0,
        tiled=True,
    ).astype(jnp.float32)
    back_two, grad_gain_two = norm_back(grad_normed_two, unit_two, inverse_two, gain_mlp)
    grad_hidden = cotangent + back_two
    grad_hidden_all = lax.all_gather(grad_hidden.astype(jnp.bfloat16), "tensor", axis=0, tiled=True)
    grad_out = jnp.einsum(
        "te,td->ed", attended, grad_hidden_all, preferred_element_type=jnp.float32
    )
    grad_attended = jnp.einsum(
        "td,ed->te", grad_hidden_all, w_out, preferred_element_type=jnp.float32
    )
    grad_attended = grad_attended.astype(jnp.bfloat16).reshape(
        blocks, block_rows, local_heads, HEAD_DIM
    )

    def backward_block(running, block_item):
        grad_keys, grad_values = running
        query_blk, ids_blk, grad_blk, log_blk = block_item
        scores, same_seq = block_scores(query_blk, ids_blk)
        weights = jnp.where(same_seq, jnp.exp(scores - log_blk[..., None]), 0.0)
        grad_weights = jnp.einsum(
            "qhd,khd->hqk", grad_blk, value_rows, preferred_element_type=jnp.float32
        )
        inner = jnp.sum(weights * grad_weights, axis=-1, keepdims=True)
        grad_scores = (weights * (grad_weights - inner)).astype(jnp.bfloat16)
        grad_values = grad_values + jnp.einsum(
            "hqk,qhd->khd",
            weights.astype(jnp.bfloat16),
            grad_blk,
            preferred_element_type=jnp.float32,
        )
        grad_keys = (
            grad_keys
            + jnp.einsum("hqk,qhd->khd", grad_scores, query_blk, preferred_element_type=jnp.float32)
            * scale_factor
        )
        grad_query = (
            jnp.einsum("hqk,khd->qhd", grad_scores, key_rows, preferred_element_type=jnp.float32)
            * scale_factor
        )
        return ((grad_keys, grad_values), grad_query)

    zero_rows = jnp.zeros((group_rows, local_heads, HEAD_DIM), jnp.float32)
    (grad_keys, grad_values), grad_queries = lax.scan(
        backward_block, (zero_rows, zero_rows), (query_blocks, id_blocks, grad_attended, log_totals)
    )
    grad_queries = grad_queries.reshape(group_rows, local_heads, HEAD_DIM)
    grad_projected = (
        jnp.stack(
            [
                rotate_back(grad_queries, cosine_tab, sine_tab),
                rotate_back(grad_keys, cosine_tab, sine_tab),
                grad_values,
            ]
        )
        .reshape(3, group_rows, local_width)
        .astype(jnp.bfloat16)
    )
    grad_qkv = jnp.einsum(
        "td,cte->cde", normed_all, grad_projected, preferred_element_type=jnp.float32
    )
    piece = grad_projected
    grad_normed_one = lax.psum_scatter(
        jnp.einsum("cte,cde->td", piece, w_qkv, preferred_element_type=jnp.float32).astype(
            jnp.bfloat16
        ),
        "tensor",
        scatter_dimension=0,
        tiled=True,
    ).astype(jnp.float32)
    back_one, grad_gain_one = norm_back(grad_normed_one, unit_one, inverse_one, gain_attn)
    grad_tokens = grad_hidden + back_one
    grad_qkv, grad_out, grad_gu, grad_down, grad_gain_one, grad_gain_two = lax.psum(
        (grad_qkv, grad_out, grad_gu, grad_down, grad_gain_one, grad_gain_two), "dp"
    )
    grad_gain_one, grad_gain_two = lax.psum((grad_gain_one, grad_gain_two), "tensor")
    return (
        output,
        grad_tokens,
        grad_gain_one,
        grad_gain_two,
        grad_qkv,
        grad_out,
        grad_gu,
        grad_down,
    )


def solution(mesh):
    in_specs = (
        P(("dp", "tensor"), None),
        P("dp"),
        P(),
        P(),
        P(None, None, "tensor"),
        P("tensor", None),
        P(None, None, "tensor"),
        P("tensor", None),
        P(("dp", "tensor"), None),
    )
    out_specs = (
        P(("dp", "tensor"), None),
        P(("dp", "tensor"), None),
        P(),
        P(),
        P(None, None, "tensor"),
        P("tensor", None),
        P(None, None, "tensor"),
        P("tensor", None),
    )
    return jax.shard_map(shards, mesh=mesh, in_specs=in_specs, out_specs=out_specs, check_vma=False)
```

profile of v0, /device:TPU:0, one launch (start us, length us, event | category | flops | bytes accessed | tf_op | source)
XLA Modules:
  0.0 787.4 jit_solution(18291366108461145955)
XLA Ops:
  18.8 23.3 %all-gather.5.cloned.1.call-done = bf16[2048,768]{1,0:T(8,128)(2,1)} async-done(((bf16[512,768]{1,0:T(8,128)(2,1)}), bf16[2048,768]{1,0:T(8,128)(2,1)}) %all-gather.5.cloned.1.call-update) | async-done | bytes 3145744 | tf_op jit(solution)/shard_map/all_gather | solution.py:81
  60.9 84.4 %while.27 = (s32[]{:T(128)}, bf16[4,512,3,64]{1,3,2,0:T(8,128)(2,1)}, f32[4,3,512]{2,1,0:T(4,128)}, s32[4,512]{1,0:T(4,128)S(1)}, s32[2048]{0:T(1024)S(1)}, /*in...) while((s32[]{:T(128)}, ...), condition=%wide.region_7.8_spmd, body=%wide.region_4.7_spmd.sunk | while | flops 844102144 | bytes 50466988 | solution.py:111
  61.9 5.9 fusion.142
  67.8 6.8 fusion.143
  74.7 6.7 fusion.144
  82.9 5.9 fusion.142
  88.9 6.8 fusion.143
  95.7 6.7 fusion.144
  104.0 5.9 fusion.142
  109.9 6.8 fusion.143
  116.7 6.7 fusion.144
  125.0 5.9 fusion.142
  130.9 6.8 fusion.143
  137.8 6.7 fusion.144
  151.6 38.1 %reduce-scatter.5.cloned.1.call-done = bf16[512,768]{1,0:T(8,128)(2,1)} async-done(((bf16[2048,768]{1,0:T(8,128)(2,1)}), bf16[512,768]{1,0:T(8,128)(2,1)}) %reduce-scatter.5.cloned.1.call-update) | async-done | bytes 786448 | tf_op jit(solution)/shard_map/reduce_scatter | solution.py:114
  195.5 27.1 %all-gather.7.cloned.1.call-done = bf16[2048,768]{1,0:T(8,128)(2,1)} async-done(((bf16[512,768]{1,0:T(8,128)(2,1)}), bf16[2048,768]{1,0:T(8,128)(2,1)}) %all-gather.7.cloned.1.call-update) | async-done | bytes 3145744 | tf_op jit(solution)/shard_map/all_gather | solution.py:122
  222.6 6.3 convolution_bitcast_fusion
  228.9 24.4 %all-gather.9.cloned.1.call-done = bf16[2048,768]{1,0:T(8,128)(2,1)} async-done(((bf16[512,768]{1,0:T(8,128)(2,1)}), bf16[2048,768]{1,0:T(8,128)(2,1)}) %all-gather.9.cloned.1.call-update) | async-done | bytes 3145744 | tf_op jit(solution)/shard_map/all_gather | solution.py:134
  253.2 6.0 fusion.81
  260.7 4.1 bitcast_convert_fusion.1
  264.8 12.0 %reduce-scatter.7.cloned.1.call-start = ((), (), s32[]{:S(2)}) async-start(), calls=%async_computation.7 | async-start | bytes 3932160 | tf_op jit(solution)/shard_map/reduce_scatter | solution.py:127
  276.8 4.8 convolution_convert_fusion
  281.7 21.3 %reduce-scatter.9.cloned.1.call-done = bf16[512,768]{1,0:T(8,128)(2,1)} async-done(((bf16[2048,768]{1,0:T(8,128)(2,1)}), bf16[512,768]{1,0:T(8,128)(2,1)}) %reduce-scatter.9.cloned.1.call-update) | async-done | bytes 786448 | tf_op jit(solution)/shard_map/reduce_scatter | solution.py:144
  306.7 36.7 %reduce-scatter.7.cloned.1.call-done = bf16[512,768]{1,0:T(8,128)(2,1)} async-done(((bf16[2048,768]{1,0:T(8,128)(2,1)}), bf16[512,768]{1,0:T(8,128)(2,1)}) %reduce-scatter.7.cloned.1.call-update) | async-done | bytes 786448 | tf_op jit(solution)/shard_map/reduce_scatter | solution.py:127
  343.3 4.5 fusion.90
  347.9 28.6 %all-gather.11.cloned.1.call-done = bf16[2048,768]{1,0:T(8,128)(2,1)} async-done(((bf16[512,768]{1,0:T(8,128)(2,1)}), bf16[2048,768]{1,0:T(8,128)(2,1)}) %all-gather.11.cloned.1.call-update) | async-done | bytes 3145744 | tf_op jit(solution)/shard_map/all_gather | solution.py:154
  385.6 150.5 %while.28 = (s32[]{:T(128)}, f32[2048,3,64]{0,2,1:T(8,128)S(1)}, f32[2048,3,64]{0,2,1:T(8,128)}, f32[4,512,3,64]{1,0,3,2:T(4,128)}, bf16[4,512,3,64]{1,3,2,0:T(8...) while((s32[]{:T(128)}, f32[2048,3,64]{0,2,1:T(8,128)S(1)}, ...), condition=%wide.region_17.18_spmd.clone, body=%wide.region_15.17_spmd.clone.sunk | while | flops 2063563264 | bytes 116322528 | solution.py:193
  389.9 4.1 fusion.156
  393.9 7.2 multiply_reduce_fusion.4
  401.2 6.8 multiply_convert_fusion.6
  413.5 8.6 %dynamic_update_slice.19 = f32[4,512,3,64]{1,0,3,2:T(4,128)} dynamic-update-slice(f32[4,512,3,64]{1,0,3,2:T(4,128)} %get-tuple-element.430, f32[1,512,3,64]{1,0,3,2:T(1,128)} %copy.42, s32[]{:T(128)S(6)} %copy.59, s32[]{:T(128)} %constant.50.clone.1..sunk, s32[]{:T(128)} %constant.50.clone.1..sunk, s32[]{:T(128)} %constant.50.clone.1..sunk) | dynamic-update-slice | bytes 786436 | tf_op jit(solution)/shard_map/while/body/jit(dynamic_update_index_in_dim)/dynamic_update_slice | solution.py:111
  426.4 5.6 fusion.156
  431.9 7.2 multiply_reduce_fusion.4
  439.2 6.8 multiply_convert_fusion.6
  451.5 8.6 %dynamic_update_slice.19 = f32[4,512,3,64]{1,0,3,2:T(4,128)} dynamic-update-slice(f32[4,512,3,64]{1,0,3,2:T(4,128)} %get-tuple-element.430, f32[1,512,3,64]{1,0,3,2:T(1,128)} %copy.42, s32[]{:T(128)S(6)} %copy.59, s32[]{:T(128)} %constant.50.clone.1..sunk, s32[]{:T(128)} %constant.50.clone.1..sunk, s32[]{:T(128)} %constant.50.clone.1..sunk) | dynamic-update-slice | bytes 786436 | tf_op jit(solution)/shard_map/while/body/jit(dynamic_update_index_in_dim)/dynamic_update_slice | solution.py:111
  464.4 5.6 fusion.156
  469.9 7.2 multiply_reduce_fusion.4
  477.2 6.8 multiply_convert_fusion.6
  489.5 8.6 %dynamic_update_slice.19 = f32[4,512,3,64]{1,0,3,2:T(4,128)} dynamic-update-slice(f32[4,512,3,64]{1,0,3,2:T(4,128)} %get-tuple-element.430, f32[1,512,3,64]{1,0,3,2:T(1,128)} %copy.42, s32[]{:T(128)S(6)} %copy.59, s32[]{:T(128)} %constant.50.clone.1..sunk, s32[]{:T(128)} %constant.50.clone.1..sunk, s32[]{:T(128)} %constant.50.clone.1..sunk) | dynamic-update-slice | bytes 786436 | tf_op jit(solution)/shard_map/while/body/jit(dynamic_update_index_in_dim)/dynamic_update_slice | solution.py:111
  502.4 5.6 fusion.156
  507.9 7.2 multiply_reduce_fusion.4
  515.2 6.8 multiply_convert_fusion.6
  527.5 8.6 %dynamic_update_slice.19 = f32[4,512,3,64]{1,0,3,2:T(4,128)} dynamic-update-slice(f32[4,512,3,64]{1,0,3,2:T(4,128)} %get-tuple-element.430, f32[1,512,3,64]{1,0,3,2:T(1,128)} %copy.42, s32[]{:T(128)S(6)} %copy.59, s32[]{:T(128)} %constant.50.clone.1..sunk, s32[]{:T(128)} %constant.50.clone.1..sunk, s32[]{:T(128)} %constant.50.clone.1..sunk) | dynamic-update-slice | bytes 786436 | tf_op jit(solution)/shard_map/while/body/jit(dynamic_update_index_in_dim)/dynamic_update_slice | solution.py:111
  548.5 4.0 bitcast_convert_fusion
  566.3 24.4 %reduce-scatter.11.cloned.1.call-done = bf16[512,768]{1,0:T(8,128)(2,1)} async-done(((bf16[2048,768]{1,0:T(8,128)(2,1)}), bf16[512,768]{1,0:T(8,128)(2,1)}) %reduce-scatter.11.cloned.1.call-update) | async-done | bytes 786448 | tf_op jit(solution)/shard_map/reduce_scatter | solution.py:212
  592.7 22.2 %all-reduce = (f32[768]{0:T(1024)S(1)}, f32[768]{0:T(1024)S(1)}) all-reduce(f32[768]{0:T(1024)S(1)} %get-tuple-element.183, f32[768]{0:T(1024)S(1)} %copy-done.44), channel_id=1, replica_groups=mesh['dp'=8,'tensor'=4] {'dp'}, use_global_device_ids=true, to_apply=%region_22.23 | all-reduce | flops 1536 | bytes 12288 | tf_op jit(solution)/shard_map/psum | solution.py:222
  614.9 6.8 all-reduce.2
  624.8 149.3 %all-reduce.5.cloned.1.call-done = (f32[3,768,192]{1,2,0:T(8,128)}, f32[192,768]{1,0:T(8,128)}, f32[2,768,288]{1,2,0:T(8,128)}, f32[288,768]{1,0:T(8,128)}) async-done(((f32[3,768,192]{1,2,0:T(8,128)}, f32[192,768]{1,0:T(8,128)}, f32[2,768,288]{1,2,0:T(8,128)}, f32[288,768]{1,0:T(8,128)}), (f32[3,768,192]{1,2,0:T(8,128)}, f32[192,768]{1,0:T(8,128)}, f32[2,768,288]{1,2,0:T(8,128)}, ...) | async-done | bytes 5013520 | tf_op jit(solution)/shard_map/psum | solution.py:222
  (264 shorter events, 138.3 us)
Async XLA Ops:
  7.2 34.9 %copy-start = (bf16[3,768,192]{1,2,0:T(8,128)(2,1)S(1)}, bf16[3,768,192]{1,2,0:T(8,128)(2,1)}, u32[]{:S(2)}) copy-start(bf16[3,768,192]{1,2,0:T(8,128)(2,1)} %param.17) | copy-start | bytes 2654212
  7.2 2.0 copy-start.1
  7.2 2.3 copy-start.39
  7.2 34.8 %all-gather.5.cloned.1.call-start = ((), (), s32[]{:S(2)}) async-start(), calls=%async_computation.4 | async-start | bytes 3932160 | tf_op jit(solution)/shard_map/all_gather | solution.py:81
  10.7 179.0 %reduce-scatter.5.cloned.1.call-start = ((), (), s32[]{:S(2)}) async-start(), calls=%async_computation.5 | async-start | bytes 3932160 | tf_op jit(solution)/shard_map/reduce_scatter | solution.py:114
  67.8 6.8 copy-start.25
  88.9 6.8 copy-start.25
  109.9 6.8 copy-start.25
  130.9 6.8 copy-start.25
  145.4 2.5 copy-start.4
  145.4 2.5 copy-start.11
  145.4 3.5 copy-start.34
  151.5 38.1 %copy-start.2 = (f32[512,768]{1,0:T(8,128)S(1)}, f32[512,768]{1,0:T(8,128)}, u32[]{:S(2)}) copy-start(f32[512,768]{1,0:T(8,128)} %param.13) | copy-start | bytes 4718596
  151.5 71.1 %all-gather.7.cloned.1.call-start = ((), (), s32[]{:S(2)}) async-start(), calls=%async_computation.6 | async-start | bytes 3932160 | tf_op jit(solution)/shard_map/all_gather | solution.py:122
  193.9 59.3 %all-gather.9.cloned.1.call-start = ((), (), s32[]{:S(2)}) async-start(), calls=%async_computation.8 | async-start | bytes 3932160 | tf_op jit(solution)/shard_map/all_gather | solution.py:134
  195.4 57.8 %copy-start.48 = (bf16[288,768]{1,0:T(8,128)(2,1)S(1)}, bf16[288,768]{1,0:T(8,128)(2,1)}, u32[]{:S(2)}) copy-start(bf16[288,768]{1,0:T(8,128)(2,1)} %param.20) | copy-start | bytes 1327108
  195.4 107.5 %reduce-scatter.9.cloned.1.call-start = ((), (), s32[]{:S(2)}) async-start(), calls=%async_computation.9 | async-start | bytes 3932160 | tf_op jit(solution)/shard_map/reduce_scatter | solution.py:144
  228.9 31.9 %copy-start.47 = (bf16[2,768,288]{1,2,0:T(8,128)(2,1)S(1)}, bf16[2,768,288]{1,2,0:T(8,128)(2,1)}, u32[]{:S(2)}) copy-start(bf16[2,768,288]{1,2,0:T(8,128)(2,1)} %param.19) | copy-start | bytes 2654212
  264.8 78.5 %reduce-scatter.7.cloned.1.call-start = ((), (), s32[]{:S(2)}) async-start(), calls=%async_computation.7 | async-start | bytes 3932160 | tf_op jit(solution)/shard_map/reduce_scatter | solution.py:127
  281.6 21.4 %copy-start.7 = (f32[512,768]{1,0:T(8,128)S(1)}, f32[512,768]{1,0:T(8,128)}, u32[]{:S(2)}) copy-start(f32[512,768]{1,0:T(8,128)} %copy-done.6) | copy-start | bytes 4718596
  281.6 94.9 %all-gather.11.cloned.1.call-start = ((), (), s32[]{:S(2)}) async-start(), calls=%async_computation.10 | async-start | bytes 3932160 | tf_op jit(solution)/shard_map/all_gather | solution.py:154
  347.8 242.8 %reduce-scatter.11.cloned.1.call-start = ((), (), s32[]{:S(2)}) async-start(), calls=%async_computation.11 | async-start | bytes 3932160 | tf_op jit(solution)/shard_map/reduce_scatter | solution.py:212
  387.0 2.8 copy-start.19
  389.8 4.1 copy-start.5
  423.5 2.8 copy-start.19
  426.4 5.6 copy-start.5
  461.5 2.8 copy-start.19
  464.4 5.6 copy-start.5
  499.5 2.8 copy-start.19
  502.4 5.6 copy-start.5
  542.6 2.0 copy-start.18
  544.3 3.2 copy-start.27
  552.5 221.5 %all-reduce.5.cloned.1.call-start = ((), (), s32[]{:S(2)}) async-start(), calls=%async_computation.12 | async-start | bytes 10027008 | tf_op jit(solution)/shard_map/psum | solution.py:222
  553.8 4.0 copy-start.46
  553.8 4.0 copy-start.51
  553.8 4.0 copy-start.53
  557.8 3.2 copy-start.10
  557.8 3.2 copy-start.20
  557.8 4.9 copy-start.45
  561.1 2.0 copy-start.32
  566.2 24.4 %copy-start.3 = (f32[512,768]{1,0:T(8,128)S(1)}, f32[512,768]{1,0:T(8,128)}, u32[]{:S(2)}) copy-start(f32[512,768]{1,0:T(8,128)} %param.13) | copy-start | bytes 4718596
  566.2 24.4 %copy-start.36 = (f32[512]{0:T(512)S(1)}, f32[512]{0:T(512)}, u32[]{:S(2)}) copy-start(f32[512]{0:T(512)} %copy-done.35) | copy-start | bytes 6148
  566.2 24.4 %copy-start.40 = (f32[768]{0:T(1024)S(1)}, f32[768]{0:T(1024)}, u32[]{:S(2)}) copy-start(f32[768]{0:T(1024)} %param.15) | copy-start | bytes 9220
  566.2 24.4 %copy-start.42 = (f32[512]{0:T(512)S(1)}, f32[512]{0:T(512)}, u32[]{:S(2)}) copy-start(f32[512]{0:T(512)} %copy-done.41) | copy-start | bytes 6148
  566.3 26.4 %copy-start.44 = (f32[768]{0:T(1024)S(1)}, f32[768]{0:T(1024)}, u32[]{:S(2)}) copy-start(f32[768]{0:T(1024)} %get-tuple-element.181) | copy-start | bytes 9220
  590.7 31.0 %copy-start.21 = (bf16[512,768]{1,0:T(8,128)(2,1)S(1)}, bf16[512,768]{1,0:T(8,128)(2,1)}, u32[]{:S(2)}) copy-start(bf16[512,768]{1,0:T(8,128)(2,1)} %reduce-scatter.11.cloned.1.call-done) | copy-start | bytes 2359300
  774.0 3.0 copy-start.33
  774.0 3.8 copy-start.22
  (27 other events, 33.6 us)
Sparse Core Ops, SparseCore 0:
  10.8 31.2 all-gather.4
  151.6 37.9 reduce-scatter.4
  194.0 28.5 all-gather.6
  224.7 28.5 all-gather.8
  265.0 37.9 reduce-scatter.8
  305.4 37.9 reduce-scatter.6
  348.0 28.5 all-gather.10
  552.7 37.9 reduce-scatter.10
  595.2 178.7 all-reduce.4
where the time goes:
time: 796 us; the launch traced here: 787 us
  waiting for transfers between devices  373 us (47%)
  matrix products  177 us (22%)
  other arithmetic  97.5 us (12%)
  local copies, waits for them, and re-layouts  82.8 us (10%)
  blocking collectives  29 us (4%)
  between operations  15.3 us (2%)
  starting transfers between devices  12.3 us (2%)
    psum x1, waiting for transfers between devices, shards(): lax.psum((grad_qkv, grad_out, grad_gu, grad_down, grad_gain_one, grad_gai...  149 us
    dynamic_update_slice x8, local copies, waits for them, and re-layouts, shards(): attended, log_totals = lax.map(forward_block, (query_blocks, id_blocks))  39.1 us
    reduce_scatter x1, waiting for transfers between devices, shards(): lax.psum_scatter(jnp.dot(piece, w_out, preferred_element_type=jnp.float32...  38.1 us
    reduce_scatter x1, waiting for transfers between devices, shards(): lax.psum_scatter(jnp.dot(piece, w_down, preferred_element_type=jnp.float3...  36.7 us
    dot_general x8, matrix products, block_scores(): jnp.einsum('qhd,khd->hqk', query_blk, key_rows, preferred_element_type=jn...  35.1 us
    dot_general x4, matrix products, backward_block(): jnp.einsum('qhd,khd->hqk', grad_blk, value_rows, preferred_element_type=j...  28.9 us
    all_gather x1, waiting for transfers between devices, shards(): lax.all_gather(grad_hidden.astype(jnp.bfloat16), 'tensor', axis=0, tiled=...  28.6 us
    convert_element_type x4, other arithmetic, backward_block(): grad_scores = (weights * (grad_weights - inner)).astype(jnp.bfloat16)  27.3 us
  transfers between devices with their start and end apart: 9, of which 9 were waited for; matrix products, arithmetic and copies ran while one was open for 5% of the time, Pallas kernels for 0%

commit v1 on v0

v1 whole, which is shorter than its diff:
```python
import functools

import jax
import jax.numpy as jnp
from jax import lax
from jax.experimental import pallas as pl
from jax.experimental.pallas import tpu as pltpu
from jax.sharding import PartitionSpec as P

HEAD_DIM = 64


EPSILON = 1e-05
ROPE_BASE = 160000.0
NEG_FILL = -1e30
INV_ROOT_TWO = 0.7071067811865476
INV_ROOT_TWO_PI = 0.3989422804014327
BLOCK = 256
LAST = (((1,), (1,)), ((), ()))


def norm_rows(values, gain_vec):
    center = values - jnp.mean(values, axis=-1, keepdims=True)
    spread = jnp.mean(center * center, axis=-1, keepdims=True)
    inverse = lax.rsqrt(spread + EPSILON)
    unit_rows = center * inverse
    return (unit_rows * gain_vec, unit_rows, inverse)


def norm_back(grad_rows, unit_rows, inverse, gain_vec):
    scaled = grad_rows * gain_vec
    inner = (
        scaled
        - jnp.mean(scaled, axis=-1, keepdims=True)
        - unit_rows * jnp.mean(scaled * unit_rows, axis=-1, keepdims=True)
    )
    return inner * inverse


def gelu_parts(before_act):
    normal_cdf = 0.5 * (1.0 + lax.erf(before_act * INV_ROOT_TWO))
    density = jnp.exp(-0.5 * before_act * before_act) * INV_ROOT_TWO_PI
    return (before_act * normal_cdf, normal_cdf + before_act * density)


def turn_columns(weights):
    depth, width = weights.shape
    halves = weights.reshape(depth, width // HEAD_DIM, 2, HEAD_DIM // 2)
    return jnp.stack([-halves[:, :, 1], halves[:, :, 0]], axis=2).reshape(depth, width)


def head_rows(rows, head):
    row = lax.broadcasted_iota(jnp.int32, rows.shape, 0)
    inside = (row >= head * HEAD_DIM) & (row < (head + 1) * HEAD_DIM)
    return jnp.where(inside, rows, jnp.zeros_like(rows))


def forward_kernel(
    heads, low_ref, high_ref, idr_ref, idc_ref, q_ref, k_ref, vt_ref, out_ref, log_ref, acc_ref
):
    block = pl.program_id(0)
    ids = idr_ref[...]
    query_t = q_ref[...]
    masked = [head_rows(query_t, head) for head in range(heads)]
    acc_ref[...] = jnp.zeros_like(acc_ref)

    def step(at, carry):
        start = pl.multiple_of(at * BLOCK, BLOCK)
        keys = k_ref[pl.ds(start, BLOCK), :]
        same = idc_ref[pl.ds(start, BLOCK), :] == ids
        result = []
        for head in range(heads):
            top, total = carry[head]
            scores = jnp.dot(keys, masked[head], preferred_element_type=jnp.float32)
            scores = jnp.where(same, scores, NEG_FILL)
            new_top = jnp.maximum(top, jnp.max(scores, axis=0, keepdims=True))
            fade = jnp.exp(top - new_top)
            weights = jnp.exp(scores - new_top)
            total = total * fade + jnp.sum(weights, axis=0, keepdims=True)
            rows = pl.ds(head * HEAD_DIM, HEAD_DIM)
            acc_ref[rows, :] = acc_ref[rows, :] * fade + jnp.dot(
                vt_ref[rows, pl.ds(start, BLOCK)],
                weights.astype(jnp.bfloat16),
                preferred_element_type=jnp.float32,
            )
            result.append((new_top, total))
        return tuple(result)

    first = tuple(
        (jnp.full((1, BLOCK), NEG_FILL, jnp.float32), jnp.zeros((1, BLOCK), jnp.float32))
        for _ in range(heads)
    )
    final = lax.fori_loop(low_ref[block], high_ref[block], step, first)
    for head in range(heads):
        top, total = final[head]
        rows = pl.ds(head * HEAD_DIM, HEAD_DIM)
        out_ref[0, rows, :] = (acc_ref[rows, :] / total).astype(jnp.bfloat16)
        log_ref[head : head + 1, :] = top + jnp.log(total)


def backward_kernel(
    heads,
    low_ref,
    high_ref,
    idr_ref,
    idc_ref,
    q_ref,
    g_ref,
    o_ref,
    log_ref,
    k_ref,
    kt_ref,
    v_ref,
    dq_ref,
    dk_ref,
    dv_ref,
    acc_ref,
):
    block = pl.program_id(0)

    @pl.when(block == 0)
    def _():
        dk_ref[...] = jnp.zeros_like(dk_ref)
        dv_ref[...] = jnp.zeros_like(dv_ref)

    ids = idr_ref[...]
    query_t = q_ref[...]
    grad_t = g_ref[0]
    product = grad_t.astype(jnp.float32) * o_ref[0].astype(jnp.float32)
    masked_q = [head_rows(query_t, head) for head in range(heads)]
    masked_g = [head_rows(grad_t, head) for head in range(heads)]
    inner = [
        jnp.sum(product[head * HEAD_DIM : (head + 1) * HEAD_DIM], axis=0, keepdims=True)
        for head in range(heads)
    ]
    logs = [log_ref[head : head + 1, :] for head in range(heads)]
    acc_ref[...] = jnp.zeros_like(acc_ref)

    def step(at, carry):
        start = pl.multiple_of(at * BLOCK, BLOCK)
        columns = pl.ds(start, BLOCK)
        keys = k_ref[columns, :]
        values = v_ref[columns, :]
        same = idc_ref[columns, :] == ids
        for head in range(heads):
            rows = pl.ds(head * HEAD_DIM, HEAD_DIM)
            scores = jnp.dot(keys, masked_q[head], preferred_element_type=jnp.float32)
            weights = jnp.exp(jnp.where(same, scores - logs[head], NEG_FILL))
            grad_w = jnp.dot(values, masked_g[head], preferred_element_type=jnp.float32)
            grad_s = (weights * (grad_w - inner[head])).astype(jnp.bfloat16)
            dv_ref[rows, columns] += lax.dot_general(
                g_ref[0, rows, :],
                weights.astype(jnp.bfloat16),
                LAST,
                preferred_element_type=jnp.float32,
            )
            dk_ref[rows, columns] += lax.dot_general(
                q_ref[rows, :], grad_s, LAST, preferred_element_type=jnp.float32
            )
            acc_ref[rows, :] += jnp.dot(
                kt_ref[rows, columns], grad_s, preferred_element_type=jnp.float32
            )
        return carry

    lax.fori_loop(low_ref[block], high_ref[block], step, 0)
    dq_ref[...] = acc_ref[...] * (HEAD_DIM**-0.5)


def attend(low, high, id_row, id_column, query_t, keys, value_t, parts):
    width, length = query_t.shape
    heads = width // HEAD_DIM
    per_part = length // parts // BLOCK
    grid_spec = pltpu.PrefetchScalarGridSpec(
        num_scalar_prefetch=2,
        grid=(length // BLOCK,),
        in_specs=[
            pl.BlockSpec((1, BLOCK), lambda i, *_: (0, i)),
            pl.BlockSpec((length, 1), lambda i, *_: (0, 0)),
            pl.BlockSpec((width, BLOCK), lambda i, *_: (0, i)),
            pl.BlockSpec((length, width), lambda i, *_: (0, 0)),
            pl.BlockSpec((width, length), lambda i, *_: (0, 0)),
        ],
        out_specs=[
            pl.BlockSpec((1, width, BLOCK), lambda i, *_: (i // per_part, 0, i % per_part)),
            pl.BlockSpec((heads, BLOCK), lambda i, *_: (0, i)),
        ],
        scratch_shapes=[pltpu.VMEM((width, BLOCK), jnp.float32)],
    )
    return pl.pallas_call(
        functools.partial(forward_kernel, heads),
        grid_spec=grid_spec,
        out_shape=[
            jax.ShapeDtypeStruct((parts, width, length // parts), jnp.bfloat16),
            jax.ShapeDtypeStruct((heads, length), jnp.float32),
        ],
        compiler_params=pltpu.CompilerParams(
            dimension_semantics=("arbitrary",), vmem_limit_bytes=32 * 1024 * 1024
        ),
        cost_estimate=pl.CostEstimate(
            flops=4 * length * length * width,
            bytes_accessed=10 * length * width,
            transcendentals=heads * length * length,
        ),
        name="attend",
    )(low, high, id_row, id_column, query_t, keys, value_t)


def attend_back(
    low, high, id_row, id_column, query_t, grad_t, out_t, logs, keys, key_t, values, parts
):
    width, length = query_t.shape
    heads = width // HEAD_DIM
    per_part = length // parts // BLOCK
    part_spec = pl.BlockSpec((1, width, BLOCK), lambda i, *_: (i // per_part, 0, i % per_part))
    whole_rows = pl.BlockSpec((length, width), lambda i, *_: (0, 0))
    whole_columns = pl.BlockSpec((width, length), lambda i, *_: (0, 0))
    some_columns = pl.BlockSpec((width, BLOCK), lambda i, *_: (0, i))
    grid_spec = pltpu.PrefetchScalarGridSpec(
        num_scalar_prefetch=2,
        grid=(length // BLOCK,),
        in_specs=[
            pl.BlockSpec((1, BLOCK), lambda i, *_: (0, i)),
            pl.BlockSpec((length, 1), lambda i, *_: (0, 0)),
            some_columns,
            part_spec,
            part_spec,
            pl.BlockSpec((heads, BLOCK), lambda i, *_: (0, i)),
            whole_rows,
            whole_columns,
            whole_rows,
        ],
        out_specs=[some_columns, whole_columns, whole_columns],
        scratch_shapes=[pltpu.VMEM((width, BLOCK), jnp.float32)],
    )
    return pl.pallas_call(
        functools.partial(backward_kernel, heads),
        grid_spec=grid_spec,
        out_shape=[jax.ShapeDtypeStruct((width, length), jnp.float32)] * 3,
        compiler_params=pltpu.CompilerParams(
            dimension_semantics=("arbitrary",), vmem_limit_bytes=32 * 1024 * 1024
        ),
        cost_estimate=pl.CostEstimate(
            flops=10 * length * length * width,
            bytes_accessed=24 * length * width,
            transcendentals=heads * length * length,
        ),
        name="attend_back",
    )(low, high, id_row, id_column, query_t, grad_t, out_t, logs, keys, key_t, values)


def turn_back_rows(grad_t, cosine_t, sine_t):
    width, length = grad_t.shape
    half = HEAD_DIM // 2
    split = grad_t.reshape(width // HEAD_DIM, 2, half, length)
    first, second = split[:, 0], split[:, 1]
    return jnp.stack(
        [first * cosine_t + second * sine_t, second * cosine_t - first * sine_t], axis=1
    ).reshape(width, length)


def shards(tokens, seq_ids, gain_attn, gain_mlp, w_qkv, w_out, w_gu, w_down, cotangent):
    f32, bf16 = jnp.float32, jnp.bfloat16
    dot = functools.partial(jnp.einsum, preferred_element_type=f32)
    length = seq_ids.shape[0]
    model = tokens.shape[1]
    width = w_out.shape[0]
    heads = width // HEAD_DIM
    hidden = w_down.shape[0]
    parts = length // tokens.shape[0]
    normed_one, unit_one, inverse_one = norm_rows(tokens, gain_attn)
    normed_all = lax.all_gather(normed_one.astype(bf16), "tensor", axis=0, tiled=True)
    before = jnp.sum((seq_ids[None, :] < seq_ids[:, None]).astype(jnp.int32), axis=1)
    places = (jnp.arange(length, dtype=jnp.int32) - before).astype(f32)
    half = HEAD_DIM // 2
    frequency = ROPE_BASE ** (-(jnp.arange(half, dtype=f32) * 2.0) / HEAD_DIM)
    angles = frequency[:, None] * places[None, :]
    cosine_t, sine_t = jnp.cos(angles), jnp.sin(angles)
    cosine_wide, sine_wide = jnp.tile(cosine_t, (2 * heads, 1)), jnp.tile(sine_t, (2 * heads, 1))
    low = before[::BLOCK] // BLOCK
    last_ids = seq_ids[BLOCK - 1 :: BLOCK]
    upto = jnp.sum((seq_ids[None, :] <= last_ids[:, None]).astype(jnp.int32), axis=1)
    high = (upto + (BLOCK - 1)) // BLOCK
    id_row, id_column = seq_ids[None, :], seq_ids[:, None]
    w_q, w_k, w_v = w_qkv[0], w_qkv[1], w_qkv[2]
    w_all = jnp.concatenate([w_q, w_k, w_v, turn_columns(w_q), turn_columns(w_k)], axis=1)
    projected = dot("de,td->et", w_all, normed_all)
    q_t, k_t, v_t, q_turn, k_turn = [
        projected[i * width : (i + 1) * width] for i in range(5)
    ]
    query_t = ((q_t * cosine_wide + q_turn * sine_wide) * HEAD_DIM**-0.5).astype(bf16)
    key_t = (k_t * cosine_wide + k_turn * sine_wide).astype(bf16)
    value_t = v_t.astype(bf16)
    keys, values = key_t.T, value_t.T
    out_t, logs = attend(low, high, id_row, id_column, query_t, keys, value_t, parts)
    _, s_out, s_gate, s_up, s_down = lax.optimization_barrier(
        (normed_all, w_out, w_gu[0].T, w_gu[1].T, w_down)
    )
    a_out, a_gate, a_up, a_down = [
        lax.all_gather(w, "tensor", axis=0, tiled=True) for w in (s_out, s_gate, s_up, s_down)
    ]
    att_t = lax.all_to_all(out_t, "tensor", 0, 0).reshape(parts * width, tokens.shape[0])
    hidden_in = tokens + dot("et,ed->td", att_t, a_out)
    normed_two, unit_two, inverse_two = norm_rows(hidden_in, gain_mlp)
    normed_two = normed_two.astype(bf16)
    gate = dot("td,fd->tf", normed_two, a_gate)
    up = dot("td,fd->tf", normed_two, a_up)
    gelu_value, gelu_slope = gelu_parts(gate)
    activated = (gelu_value * up).astype(bf16)
    output = hidden_in + dot("tf,fd->td", activated, a_down)
    grad_two = cotangent.astype(bf16)
    grad_act = dot("td,fd->tf", grad_two, a_down)
    grad_gate = (grad_act * up * gelu_slope).astype(bf16)
    grad_up = (grad_act * gelu_value).astype(bf16)
    grad_normed_two = dot("tf,fd->td", grad_gate, a_gate) + dot("tf,fd->td", grad_up, a_up)
    grad_hidden = cotangent + norm_back(grad_normed_two, unit_two, inverse_two, gain_mlp)
    grad_gain_two = jnp.sum(grad_normed_two * unit_two, axis=0)
    grad_one = grad_hidden.astype(bf16)
    grad_att_t = dot("ed,td->et", a_out, grad_one).astype(bf16)
    grad_t = lax.all_to_all(
        grad_att_t.reshape(parts, width, tokens.shape[0]), "tensor", 0, 0
    )
    pieces = [
        dot("tf,td->fd", activated, grad_two).astype(bf16).reshape(parts, hidden, model),
        dot("tf,td->fd", grad_gate, normed_two).astype(bf16).reshape(parts, hidden, model),
        dot("tf,td->fd", grad_up, normed_two).astype(bf16).reshape(parts, hidden, model),
        dot("et,td->ed", att_t, grad_one).astype(bf16).reshape(parts, width, model),
    ]
    stacked = jnp.concatenate(pieces, axis=1)
    stacked, grad_t = lax.optimization_barrier((stacked, grad_t))
    mine = lax.psum_scatter(stacked, "tensor", scatter_dimension=0, tiled=False)
    summed = lax.psum(mine, "dp")
    dq_t, dk_t, dv_t = attend_back(
        low, high, id_row, id_column, query_t, grad_t, out_t, logs, keys, key_t, values, parts
    )
    grad_proj_t = jnp.concatenate(
        [
            turn_back_rows(dq_t, cosine_t, sine_t).astype(bf16),
            turn_back_rows(dk_t, cosine_t, sine_t).astype(bf16),
            dv_t.astype(bf16),
        ],
        axis=0,
    )
    w_flat = jnp.concatenate([w_q, w_k, w_v], axis=1)
    grad_normed_one = lax.psum_scatter(
        dot("et,de->td", grad_proj_t, w_flat).astype(bf16),
        "tensor",
        scatter_dimension=0,
        tiled=True,
    ).astype(f32)
    grad_qkv = dot("td,et->de", normed_all, grad_proj_t)
    grad_gain_one = jnp.sum(grad_qkv * w_flat.astype(f32), axis=1) / gain_attn
    sent, summed = lax.optimization_barrier((grad_qkv.astype(bf16), summed))
    grad_qkv = lax.psum(sent, "dp").astype(f32)
    grad_qkv = jnp.stack([grad_qkv[:, i * width : (i + 1) * width] for i in range(3)])
    gains = lax.psum(jnp.stack([grad_gain_one, grad_gain_two]), ("dp", "tensor"))
    grad_tokens = grad_hidden + norm_back(grad_normed_one, unit_one, inverse_one, gain_attn)
    summed = summed.astype(f32)
    grad_down = summed[:hidden]
    grad_gu = jnp.stack([summed[hidden : 2 * hidden].T, summed[2 * hidden : 3 * hidden].T])
    grad_out = summed[3 * hidden :]
    return (
        output,
        grad_tokens,
        gains[0],
        gains[1],
        grad_qkv,
        grad_out,
        grad_gu,
        grad_down,
    )


def solution(mesh):
    in_specs = (
        P(("dp", "tensor"), None),
        P("dp"),
        P(),
        P(),
        P(None, None, "tensor"),
        P("tensor", None),
        P(None, None, "tensor"),
        P("tensor", None),
        P(("dp", "tensor"), None),
    )
    out_specs = (
        P(("dp", "tensor"), None),
        P(("dp", "tensor"), None),
        P(),
        P(),
        P(None, None, "tensor"),
        P("tensor", None),
        P(None, None, "tensor"),
        P("tensor", None),
    )
    return jax.shard_map(shards, mesh=mesh, in_specs=in_specs, out_specs=out_specs, check_vma=False)
```

time: 796 us -> 456 us (0.57)
  waiting for transfers between devices: 373 us -> 208 us
  matrix products: 177 us -> 45.1 us
  Pallas kernels: 0 us -> 78.9 us
  other arithmetic: 97.5 us -> 25.4 us
  local copies, waits for them, and re-layouts: 82.8 us -> 18.8 us
  blocking collectives: 29 us -> 59 us
    dot_general x39 -> x15, matrix products: 173 us -> 45.1 us  [the longest x1 5.37 us: shards(): grad_act = dot('td,fd->tf', grad_two, a_down)]
    reduce_scatter x4 -> x2, waiting for transfers between devices: 120 us -> 8.16 us  [the longest x1 8.16 us: shards(): mine = lax.psum_scatter(stacked, 'tensor', scatter_dimension=0, tiled=False)]
    pallas_call x0 -> x2, Pallas kernels: none -> 78.9 us  [the longest x1 39.8 us: attend_back(): pl.pallas_call(functools.partial(backward_kernel, heads), grid_spec=grid_...]
    all_gather x4 -> x5, waiting for transfers between devices: 103 us -> 36.2 us  [the longest x1 30.3 us: shards(): lax.all_gather(normed_one.astype(bf16), 'tensor', axis=0, tiled=True)]
    dynamic_update_slice x8 -> x0, local copies, waits for them, and re-layouts: 39.1 us -> none  [shards(): attended, log_totals = lax.map(forward_block, (query_blocks, id_blocks))]
    convert_element_type x12 -> x7, other arithmetic: 37.8 us -> 4.71 us  [the longest x1 1.29 us: shards(): grad_qkv = lax.psum(sent, 'dp').astype(f32)]
    reduce_sum x6 -> x3, other arithmetic: 31.8 us -> 3.85 us  [the longest x1 1.85 us: norm_back(): jnp.mean(scaled, axis=-1, keepdims=True)]
    all_to_all x0 -> x1, blocking collectives: none -> 19.6 us  [shards(): lax.all_to_all(out_t, 'tensor', 0, 0)]
  transfers between devices with their start and end apart: 9 -> 10, of which waited for: 9 -> 6; matrix products, arithmetic and copies ran while one was open for 5% -> 12% of each run, Pallas kernels for 0% -> 17%
where the time goes in v1:
time: 456 us; the launch traced here: 455 us
  waiting for transfers between devices  208 us (46%)
  Pallas kernels  78.9 us (17%)
  blocking collectives  59 us (13%)
  matrix products  45.1 us (10%)
  other arithmetic  25.4 us (6%)
  local copies, waits for them, and re-layouts  18.8 us (4%)
  between operations  14.4 us (3%)
  starting transfers between devices  4.78 us (1%)
    psum x1, waiting for transfers between devices, shards(): summed = lax.psum(mine, 'dp')  85.5 us
    psum x1, waiting for transfers between devices, shards(): grad_qkv = lax.psum(sent, 'dp').astype(f32)  72.8 us
    pallas_call x1, Pallas kernels, attend_back(): pl.pallas_call(functools.partial(backward_kernel, heads), grid_spec=grid_...  39.8 us
    psum x1, blocking collectives, shards(): lax.psum(jnp.stack([grad_gain_one, grad_gain_two]), ('dp', 'tensor'))  39.4 us
    pallas_call x1, Pallas kernels, attend(): pl.pallas_call(functools.partial(forward_kernel, heads), grid_spec=grid_s...  39.1 us
    all_gather x1, waiting for transfers between devices, shards(): lax.all_gather(normed_one.astype(bf16), 'tensor', axis=0, tiled=True)  30.3 us
    all_to_all x1, blocking collectives, shards(): lax.all_to_all(out_t, 'tensor', 0, 0)  19.6 us
    unnamed x81, local copies, waits for them, and re-layouts  12 us
  transfers between devices with their start and end apart: 10, of which 6 were waited for; matrix products, arithmetic and copies ran while one was open for 12% of the time, Pallas kernels for 17%

profile of v1, /device:TPU:0, one launch (start us, length us, event | category | flops | bytes accessed | tf_op | source)
XLA Modules:
  0.0 454.7 jit_solution(17980281637127996715)
XLA Ops:
  7.2 1.7 reduce_sum.110
  9.4 1.1 multiply_convert_fusion.3
  10.6 1.0 slice_bitcast_fusion.5
  11.6 30.3 %all-gather.6.cloned.1.call-done = bf16[2048,768]{1,0:T(8,128)(2,1)} async-done(((bf16[512,768]{1,0:T(8,128)(2,1)}), bf16[2048,768]{1,0:T(8,128)(2,1)}) %all-gather.6.cloned.1.call-update) | async-done | bytes 3145744 | tf_op jit(solution)/shard_map/all_gather | solution.py:271
  42.8 1.8 convert_reduce_fusion
  44.7 1.4 copy.37.idc_ref
  46.3 1.0 slice_bitcast_fusion.9
  47.7 1.0 multiply_cosine_fusion
  49.4 3.2 fusion.21
  54.1 1.2 copy-done.1
  55.4 39.1 %attend.1 = (bf16[4,192,512]{2,1,0:T(8,128)(2,1)S(1)}, f32[3,2048]{1,0:T(4,128)S(1)}) custom-call(s32[8]{0:T(128)S(1)} %get-tuple-element.76.low_ref, s32[8]{0:T(128)S(1)} %get-tuple-element.75.high_ref, s32[1,2048]{1,0:T(1,128)S(1)} %bitcast.101, s32[2048,1]{1,0:T(8,128)S(1)} %copy-done.1, bf16[192,2048]{1,0:T(8,128)(2,1)S(1)} %get-tuple-element.42.q_ref, ...), custom_call_target="tpu_custom_call" | custom-call | flops 3221225472 | bytes 3932160 | tf_op jit(solution)/shard_map/attend/pallas_call | solution.py:189
  94.4 19.6 %all_to_all.10 = bf16[4,192,512]{2,1,0:T(8,128)(2,1)} all-to-all(bf16[4,192,512]{2,1,0:T(8,128)(2,1)S(1)} %get-tuple-element.21.o_ref), channel_id=1, replica_groups=mesh['dp'=8,'tensor'=4] {'tensor'}, dimensions={0} | all-to-all | bytes 1572864 | tf_op jit(solution)/shard_map/all_to_all | solution.py:301
  114.0 0.9 copy-done.3
  114.9 2.9 fusion.20
  119.0 1.1 multiply_convert_fusion.2
  120.1 4.5 fusion.22
  124.6 4.4 fusion.23
  129.0 5.8 %all-gather.14.cloned.1.call-done = bf16[1152,768]{1,0:T(8,128)(2,1)} async-done(((bf16[288,768]{1,0:T(8,128)(2,1)}), bf16[1152,768]{1,0:T(8,128)(2,1)}) %all-gather.14.cloned.1.call-update) | async-done | bytes 1769488 | tf_op jit(solution)/shard_map/all_gather | solution.py:299
  134.8 5.4 %multiply_convert_fusion = (bf16[512,1152]{1,0:T(8,128)(2,1)S(1)}, bf16[512,1152]{1,0:T(8,128)(2,1)S(1)}, bf16[512,1152]{1,0:T(8,128)(2,1)S(1)}) fusion(f32[512,1152]{1,0:T(8,128)} %fusion.22, f32[512,1152]{1,0:T(8,128)} %fusion.23, bf16[1152,768]{1,0:T(8,128)(2,1)} %all-gather.14.cloned.1.call-done, f32[512,768]{1,0:T(8,128)} %param.17), kind=kOutput, calls=%fused_computation.19 | convolution fusion | flops 915800064 | bytes 11599872 | tf_op jit(solution)/shard_map/td,fd->tf/dot_general | solution.py:311
  140.2 2.3 convolution_convert_fusion
  142.5 2.3 convolution_convert_fusion.1
  144.9 1.2 fusion.24
  146.8 1.6 multiply_reduce_fusion.1
  149.6 1.8 convolution_convert_fusion.4
  151.4 2.3 convolution_convert_fusion.2
  153.7 1.7 convolution_convert_fusion.5
  155.4 4.2 all-to-all-start.1
  159.9 6.6 %pad_maximum_fusion = bf16[4,1056,768]{2,1,0:T(8,128)(2,1)} fusion(bf16[4,192,768]{2,1,0:T(8,128)(2,1)} %bitcast.105, bf16[4,288,768]{2,1,0:T(8,128)(2,1)} %bitcast.106, bf16[4,288,768]{2,1,0:T(8,128)(2,1)} %bitcast.107, bf16[4,288,768]{2,1,0:T(8,128)(2,1)} %bitcast.108), kind=kLoop, calls=%fused_computation.1 | loop fusion | flops 25952256 | bytes 12976128 | tf_op jit(solution)/shard_map/concatenate | solution.py:328
  166.5 4.8 %all-to-all-done.1.g_ref = bf16[4,192,512]{2,1,0:T(8,128)(2,1)} async-done(((bf16[4,192,512]{2,1,0:T(8,128)(2,1)}), bf16[4,192,512]{2,1,0:T(8,128)(2,1)}, u32[]{:S(2)}, u32[]{:S(2)}) %all-to-all-start.1) | async-done | bytes 786464 | tf_op jit(solution)/shard_map/all_to_all | solution.py:319
  171.4 1.3 copy.44
  172.7 1.2 copy-done
  174.0 1.2 copy-done.2
  175.2 1.1 copy-done.4
  176.3 39.8 %attend_back.1 = (f32[192,2048]{1,0:T(8,128)S(1)}, f32[192,2048]{1,0:T(8,128)S(1)}, f32[192,2048]{1,0:T(8,128)S(1)}) custom-call(s32[8]{0:T(128)S(1)} %get-tuple-element.76.low_ref, s32[8]{0:T(128)S(1)} %get-tuple-element.75.high_ref, s32[1,2048]{1,0:T(1,128)S(1)} %bitcast.102, s32[2048,1]{1,0:T(8,128)S(1)} %copy-done.2, ...), custom_call_target="tpu_custom_call" | custom-call | flops 8053063680 | bytes 9437184 | tf_op jit(solution)/shard_map/attend_back/pallas_call | solution.py:235
  218.8 4.1 convolution_convert_fusion.3
  223.0 8.2 %reduce-scatter.5.cloned.1.call-done = bf16[1,1056,768]{2,1,0:T(8,128)(2,1)} async-done(((bf16[4,1056,768]{2,1,0:T(8,128)(2,1)}), bf16[1,1056,768]{2,1,0:T(8,128)(2,1)}) %reduce-scatter.5.cloned.1.call-update) | async-done | bytes 1622032 | tf_op jit(solution)/shard_map/reduce_scatter | solution.py:330
  231.3 4.3 convolution_add_fusion.2
  235.7 2.9 fusion.19
  238.7 39.4 %psum.21 = f32[2,768]{1,0:T(2,128)S(1)} all-reduce(f32[2,768]{1,0:T(2,128)S(1)} %pad_maximum_fusion.12), channel_id=1, replica_groups=mesh['dp'=8,'tensor'=4] {'dp','tensor'}, use_global_device_ids=true, to_apply=%region_13.14 | all-reduce | flops 1536 | bytes 12288 | tf_op jit(solution)/shard_map/psum | solution.py:355
  278.7 1.8 fusion.11
  280.6 85.5 %all-reduce.3.cloned.1.call-done = bf16[1056,768]{1,0:T(8,128)(2,1)} async-done(((bf16[1056,768]{1,0:T(8,128)(2,1)}), bf16[1056,768]{1,0:T(8,128)(2,1)}) %all-reduce.3.cloned.1.call-update) | async-done | bytes 1622032 | tf_op jit(solution)/shard_map/psum | solution.py:331
  366.2 3.0 multiply_add_fusion
  369.1 0.9 slice.135
  370.2 1.0 slice.138
  371.3 1.3 pad_maximum_fusion.3
  372.6 72.8 %all-reduce.5.cloned.1.call-done = bf16[768,576]{0,1:T(8,128)(2,1)} async-done(((bf16[768,576]{0,1:T(8,128)(2,1)}), bf16[768,576]{0,1:T(8,128)(2,1)}) %all-reduce.5.cloned.1.call-update) | async-done | bytes 884752 | tf_op jit(solution)/shard_map/psum | solution.py:353
  445.4 1.3 convert_element_type.109
  446.9 1.3 pad_maximum_fusion.2
  (134 shorter events, 11.4 us)
Async XLA Ops:
  7.2 1.9 copy-start.6
  7.2 2.2 copy-start.31
  7.2 34.8 %all-gather.6.cloned.1.call-start = ((), (), s32[]{:S(2)}) async-start(), calls=%async_computation.4 | async-start | bytes 3932160 | tf_op jit(solution)/shard_map/all_gather | solution.py:271
  9.4 1.3 copy-start.22
  10.5 32.2 %copy-start.5 = (s32[2048]{0:T(1024)S(1)}, s32[2048]{0:T(1024)}, u32[]{:S(2)}) copy-start(s32[2048]{0:T(1024)} %param.10) | copy-start | bytes 24580
  10.6 35.8 %copy-start.15 = (bf16[3,768,192]{1,2,0:T(8,128)(2,1)S(1)}, bf16[3,768,192]{1,2,0:T(8,128)(2,1)}, u32[]{:S(2)}) copy-start(bf16[3,768,192]{1,2,0:T(8,128)(2,1)} %param.13) | copy-start | bytes 2654212
  10.6 104.3 %all-gather.8.cloned.1.call-start = ((), (), s32[]{:S(2)}) async-start(), calls=%async_computation.5 | async-start | bytes 1474560 | tf_op jit(solution)/shard_map/all_gather | solution.py:299
  42.0 78.1 %all-gather.10.cloned.1.call-start = ((), (), s32[]{:S(2)}) async-start(), calls=%async_computation.6 | async-start | bytes 2211840 | tf_op jit(solution)/shard_map/all_gather | solution.py:299
  42.7 81.9 %all-gather.12.cloned.1.call-start = ((), (), s32[]{:S(2)}) async-start(), calls=%async_computation.7 | async-start | bytes 2211840 | tf_op jit(solution)/shard_map/all_gather | solution.py:299
  47.4 87.4 %all-gather.14.cloned.1.call-start = ((), (), s32[]{:S(2)}) async-start(), calls=%async_computation.8 | async-start | bytes 2211840 | tf_op jit(solution)/shard_map/all_gather | solution.py:299
  47.5 1.9 copy-start.33
  49.4 3.4 copy-start.16
  49.4 3.4 copy-start.18
  54.1 1.2 copy-start.1
  114.0 0.9 copy-start.3
  117.8 1.1 copy-start.8
  117.8 1.1 copy-start.32
  134.8 5.4 %copy-start.25 = (bf16[512,768]{1,0:T(8,128)(2,1)S(1)}, bf16[512,768]{1,0:T(8,128)(2,1)}, u32[]{:S(2)}) copy-start(bf16[512,768]{1,0:T(8,128)(2,1)} %multiply_convert_fusion.2) | copy-start | bytes 2359300
  140.2 11.2 %copy-start.37 = (bf16[512,1152]{1,0:T(8,128)(2,1)}, bf16[512,1152]{1,0:T(8,128)(2,1)S(1)}, u32[]{:S(2)}) copy-start(bf16[512,1152]{1,0:T(8,128)(2,1)S(1)} %get-tuple-element.45) | copy-start | bytes 3538948
  142.5 2.3 copy-start.35
  144.9 1.4 copy-start.9
  144.9 1.9 copy-start.36
  146.8 1.7 copy-start.20
  148.5 1.1 copy-start.13
  149.6 4.1 copy-start.11
  151.4 2.3 copy-start.21
  155.4 15.9 %all-to-all-start.1 = ((bf16[4,192,512]{2,1,0:T(8,128)(2,1)}), bf16[4,192,512]{2,1,0:T(8,128)(2,1)}, u32[]{:S(2)}, u32[]{:S(2)}) async-start(bf16[4,192,512]{2,1,0:T(8,128)(2,1)} %bitcast.118), calls=%async_computation.1 | async-start | bytes 1572864 | tf_op jit(solution)/shard_map/all_to_all | solution.py:319
  159.6 71.6 %reduce-scatter.5.cloned.1.call-start = ((), (), s32[]{:S(2)}) async-start(), calls=%async_computation.10 | async-start | bytes 8110080 | tf_op jit(solution)/shard_map/reduce_scatter | solution.py:330
  171.4 107.3 %reduce-scatter.3.cloned.1.call-start = ((), (), s32[]{:S(2)}) async-start(), calls=%async_computation.9 | async-start | bytes 3932160 | tf_op jit(solution)/shard_map/reduce_scatter | solution.py:344
  172.7 1.2 copy-start
  174.0 1.2 copy-start.2
  175.2 1.1 copy-start.4
  216.2 1.0 copy-start.17
  216.2 1.0 copy-start.19
  216.3 1.6 copy-start.23
  217.7 1.0 copy-start.26
  217.7 1.0 copy-start.27
  217.7 1.1 copy-start.29
  223.0 8.3 %copy-start.10 = (f32[512,768]{1,0:T(8,128)S(1)}, f32[512,768]{1,0:T(8,128)}, u32[]{:S(2)}) copy-start(f32[512,768]{1,0:T(8,128)} %copy-done.8) | copy-start | bytes 4718596
  223.0 143.1 %all-reduce.3.cloned.1.call-start = ((), (), s32[]{:S(2)}) async-start(), calls=%async_computation.11 | async-start | bytes 3244032 | tf_op jit(solution)/shard_map/psum | solution.py:331
  231.2 214.2 %all-reduce.5.cloned.1.call-start = ((), (), s32[]{:S(2)}) async-start(), calls=%async_computation.12 | async-start | bytes 1769472 | tf_op jit(solution)/shard_map/psum | solution.py:353
  231.3 4.4 copy-start.24
  231.3 4.4 copy-start.28
  231.3 4.4 copy-start.30
  231.3 4.4 copy-start.34
  235.7 43.0 %copy-start.7 = (f32[512,768]{1,0:T(8,128)S(1)}, f32[512,768]{1,0:T(8,128)}, u32[]{:S(2)}) copy-start(f32[512,768]{1,0:T(8,128)} %param.9) | copy-start | bytes 4718596
  278.7 87.5 %copy-start.12 = (f32[512,768]{1,0:T(8,128)S(1)}, f32[512,768]{1,0:T(8,128)}, u32[]{:S(2)}) copy-start(f32[512,768]{1,0:T(8,128)} %copy-done.11) | copy-start | bytes 4718596
  366.2 3.0 copy-start.14
Sparse Core Ops, SparseCore 0:
  10.7 31.2 all-gather.5
  43.5 17.4 all-gather.7
  63.1 20.8 all-gather.9
  86.0 25.7 all-gather.11
  113.2 21.5 all-gather.13
  171.5 59.6 reduce-scatter.4
  233.9 38.1 reduce-scatter.2
  275.7 90.3 all-reduce.2
  370.2 75.2 all-reduce.4

commit v2 on v1

--- a/solution.py
+++ b/solution.py
@@ -256,6 +256,17 @@
     return jnp.stack(
         [first * cosine_t + second * sine_t, second * cosine_t - first * sine_t], axis=1
     ).reshape(width, length)
+
+
+def swap(values, distance, parts):
+    return lax.ppermute(values, "tensor", [(i, i ^ distance) for i in range(parts)])
+
+
+def sum_groups(values, groups):
+    rows, columns = values.shape
+    received = lax.all_to_all(values.reshape(groups, rows // groups, columns), "dp", 0, 0)
+    share = jnp.sum(received.astype(jnp.float32), axis=0).astype(jnp.bfloat16)
+    return lax.all_gather(share, "dp", axis=0, tiled=True)
 
 
 def shards(tokens, seq_ids, gain_attn, gain_mlp, w_qkv, w_out, w_gu, w_down, cotangent):
@@ -295,8 +306,13 @@
     _, s_out, s_gate, s_up, s_down = lax.optimization_barrier(
         (normed_all, w_out, w_gu[0].T, w_gu[1].T, w_down)
     )
-    a_out, a_gate, a_up, a_down = [
-        lax.all_gather(w, "tensor", axis=0, tiled=True) for w in (s_out, s_gate, s_up, s_down)
+    a_out = lax.all_gather(s_out, "tensor", axis=0, tiled=True)
+    shards_own = (s_gate, s_up, s_down)
+    shards_across = [swap(w, 2, parts) for w in shards_own]
+    out_t, *shards_across = lax.optimization_barrier((out_t, *shards_across))
+    a_gate, a_up, a_down = [
+        jnp.concatenate([own, across, swap(own, 1, parts), swap(across, 1, parts)], axis=0)
+        for own, across in zip(shards_own, shards_across)
     ]
     att_t = lax.all_to_all(out_t, "tensor", 0, 0).reshape(parts * width, tokens.shape[0])
     hidden_in = tokens + dot("et,ed->td", att_t, a_out)
@@ -319,19 +335,25 @@
     grad_t = lax.all_to_all(
         grad_att_t.reshape(parts, width, tokens.shape[0]), "tensor", 0, 0
     )
-    pieces = [
-        dot("tf,td->fd", activated, grad_two).astype(bf16).reshape(parts, hidden, model),
-        dot("tf,td->fd", grad_gate, normed_two).astype(bf16).reshape(parts, hidden, model),
-        dot("tf,td->fd", grad_up, normed_two).astype(bf16).reshape(parts, hidden, model),
-        dot("et,td->ed", att_t, grad_one).astype(bf16).reshape(parts, width, model),
-    ]
-    stacked = jnp.concatenate(pieces, axis=1)
-    stacked, grad_t = lax.optimization_barrier((stacked, grad_t))
-    mine = lax.psum_scatter(stacked, "tensor", scatter_dimension=0, tiled=False)
-    summed = lax.psum(mine, "dp")
+    grads_mlp = jnp.stack(
+        [
+            dot("tf,td->fd", activated, grad_two).astype(bf16).reshape(parts, hidden, model),
+            dot("tf,td->fd", grad_gate, normed_two).astype(bf16).reshape(parts, hidden, model),
+            dot("tf,td->fd", grad_up, normed_two).astype(bf16).reshape(parts, hidden, model),
+        ],
+        axis=1,
+    )
+    half_mlp = (grads_mlp[:2].astype(f32) + swap(grads_mlp[2:], 1, parts).astype(f32)).astype(bf16)
+    grads_out = dot("et,td->ed", att_t, grad_one).astype(bf16).reshape(parts, width, model)
+    gain_rows = jnp.broadcast_to(grad_gain_two.astype(bf16), (parts, 16, model))
+    grads_out = jnp.concatenate([grads_out, gain_rows], axis=1)
+    half_mlp, grads_out, grad_t = lax.optimization_barrier((half_mlp, grads_out, grad_t))
+    mlp_mine = (half_mlp[0].astype(f32) + swap(half_mlp[1], 2, parts).astype(f32)).astype(bf16)
+    out_mine = lax.psum_scatter(grads_out, "tensor", scatter_dimension=0, tiled=False)
     dq_t, dk_t, dv_t = attend_back(
         low, high, id_row, id_column, query_t, grad_t, out_t, logs, keys, key_t, values, parts
     )
+    dq_t, dk_t, dv_t, mlp_mine = lax.optimization_barrier((dq_t, dk_t, dv_t, mlp_mine))
     grad_proj_t = jnp.concatenate(
         [
             turn_back_rows(dq_t, cosine_t, sine_t).astype(bf16),
@@ -341,28 +363,37 @@
         axis=0,
     )
     w_flat = jnp.concatenate([w_q, w_k, w_v], axis=1)
-    grad_normed_one = lax.psum_scatter(
-        dot("et,de->td", grad_proj_t, w_flat).astype(bf16),
-        "tensor",
-        scatter_dimension=0,
-        tiled=True,
-    ).astype(f32)
+    product = dot("et,de->td", grad_proj_t, w_flat).astype(bf16).reshape(parts, -1, model)
+    me = lax.axis_index("tensor")
+    mine_two, across_two, other_two, cross_two = [
+        lax.dynamic_index_in_dim(product, me ^ bits, 0, keepdims=False).astype(f32)
+        for bits in (0, 2, 1, 3)
+    ]
+    across_two = (across_two + swap(cross_two.astype(bf16), 1, parts).astype(f32)).astype(bf16)
+    mine_two = mine_two + swap(other_two.astype(bf16), 1, parts).astype(f32)
+    grad_normed_one = mine_two + swap(across_two, 2, parts).astype(f32)
     grad_qkv = dot("td,et->de", normed_all, grad_proj_t)
-    grad_gain_one = jnp.sum(grad_qkv * w_flat.astype(f32), axis=1) / gain_attn
-    sent, summed = lax.optimization_barrier((grad_qkv.astype(bf16), summed))
-    grad_qkv = lax.psum(sent, "dp").astype(f32)
+    groups = lax.axis_size("dp")
+    grad_qkv = sum_groups(grad_qkv.astype(bf16), groups).astype(f32)
+    count = 3 * hidden + width + 16
+    padding = -count % (16 * groups)
+    mine = jnp.concatenate(
+        [mlp_mine.reshape(3 * hidden, model), out_mine, jnp.zeros((padding, model), bf16)]
+    )
+    summed = sum_groups(mine, groups)
+    gain_one = lax.psum(jnp.sum(grad_qkv * w_flat.astype(f32), axis=1) / gain_attn, "tensor")
     grad_qkv = jnp.stack([grad_qkv[:, i * width : (i + 1) * width] for i in range(3)])
-    gains = lax.psum(jnp.stack([grad_gain_one, grad_gain_two]), ("dp", "tensor"))
     grad_tokens = grad_hidden + norm_back(grad_normed_one, unit_one, inverse_one, gain_attn)
     summed = summed.astype(f32)
     grad_down = summed[:hidden]
     grad_gu = jnp.stack([summed[hidden : 2 * hidden].T, summed[2 * hidden : 3 * hidden].T])
-    grad_out = summed[3 * hidden :]
+    grad_out = summed[3 * hidden : 3 * hidden + width]
+    gain_two = summed[3 * hidden + width]
     return (
         output,
         grad_tokens,
-        gains[0],
-        gains[1],
+        gain_one,
+        gain_two,
         grad_qkv,
         grad_out,
         grad_gu,

time: 456 us -> 353 us (0.77)
  waiting for transfers between devices: 208 us -> 69.7 us
  local copies, waits for them, and re-layouts: 18.8 us -> 52.6 us
  starting transfers between devices: 4.78 us -> 22.9 us
  blocking collectives: 59 us -> 41.6 us
  other arithmetic: 25.4 us -> 38.6 us
  Pallas kernels: 78.9 us -> 70.5 us
  matrix products: 45.1 us -> 37.4 us
    psum x2 -> x0, waiting for transfers between devices: 158 us -> none  [the longest x1 85.5 us: shards(): summed = lax.psum(mine, 'dp')]
    all_to_all x0 -> x3, waiting for transfers between devices: none -> 42.9 us  [the longest x2 42.9 us: sum_groups(): lax.all_to_all(values.reshape(groups, rows // groups, columns), 'dp', 0, 0)]
    all_gather x0 -> x1, blocking collectives: none -> 35.4 us  [sum_groups(): return lax.all_gather(share, 'dp', axis=0, tiled=True)]
    psum x1, blocking collectives: 39.4 us -> 6.25 us  [shards(): lax.psum(jnp.sum(grad_qkv * w_flat.astype(f32), axis=1) / gain_attn, 'ten...]
    unnamed x81 -> x111, local copies, waits for them, and re-layouts: 12 us -> 36.4 us
    all_to_all x1 -> x0, blocking collectives: 19.6 us -> none  [shards(): lax.all_to_all(out_t, 'tensor', 0, 0)]
    all_to_all x0 -> x3, starting transfers between devices: none -> 13.1 us  [the longest x2 9.37 us: sum_groups(): lax.all_to_all(values.reshape(groups, rows // groups, columns), 'dp', 0, 0)]
    convert_element_type x1 -> x4, other arithmetic: 1.29 us -> 10.9 us  [the longest x1 4.65 us: shards(): (grads_mlp[:2].astype(f32) + swap(grads_mlp[2:], 1, parts).astype(f32)).a...]
  transfers between devices with their start and end apart: 10 -> 22, of which waited for: 6 -> 4; matrix products, arithmetic and copies ran while one was open for 12% -> 24% of each run, Pallas kernels for 17% -> 20%
where the time goes in v2:
time: 353 us; the launch traced here: 348 us
  Pallas kernels  70.5 us (20%)
  waiting for transfers between devices  69.7 us (20%)
  local copies, waits for them, and re-layouts  52.6 us (15%)
  blocking collectives  41.6 us (12%)
  other arithmetic  38.6 us (11%)
  matrix products  37.4 us (11%)
  starting transfers between devices  22.9 us (6%)
  between operations  14.6 us (4%)
    all_to_all x2, waiting for transfers between devices, sum_groups(): lax.all_to_all(values.reshape(groups, rows // groups, columns), 'dp', 0, 0)  42.9 us
    unnamed x111, local copies, waits for them, and re-layouts  36.4 us
    all_gather x1, blocking collectives, sum_groups(): return lax.all_gather(share, 'dp', axis=0, tiled=True)  35.4 us
    pallas_call x1, Pallas kernels, attend(): pl.pallas_call(functools.partial(forward_kernel, heads), grid_spec=grid_s...  35.3 us
    pallas_call x1, Pallas kernels, attend_back(): pl.pallas_call(functools.partial(backward_kernel, heads), grid_spec=grid_...  35.2 us
    all_gather x1, waiting for transfers between devices, shards(): lax.all_gather(normed_one.astype(bf16), 'tensor', axis=0, tiled=True)  23.6 us
    all_to_all x2, starting transfers between devices, sum_groups(): lax.all_to_all(values.reshape(groups, rows // groups, columns), 'dp', 0, 0)  9.37 us
  transfers between devices with their start and end apart: 22, of which 4 were waited for; matrix products, arithmetic and copies ran while one was open for 24% of the time, Pallas kernels for 20%

profile of v2, /device:TPU:0, one launch (start us, length us, event | category | flops | bytes accessed | tf_op | source)
XLA Modules:
  0.0 347.9 jit_solution(10227609501294657924)
XLA Ops:
  7.2 1.7 reduce_sum.134
  10.7 1.8 convert_reduce_fusion
  18.4 23.6 %all-gather.4.cloned.1.call-done = bf16[2048,768]{1,0:T(8,128)(2,1)} async-done(((bf16[512,768]{1,0:T(8,128)(2,1)}), bf16[2048,768]{1,0:T(8,128)(2,1)}) %all-gather.4.cloned.1.call-update) | async-done | bytes 3145744 | tf_op jit(solution)/shard_map/all_gather | solution.py:282
  42.3 1.7 collective-permute-start.1
  44.2 5.1 %fusion.23 = f32[960,2048]{1,0:T(8,128)S(1)} fusion(bf16[768,960]{0,1:T(8,128)(2,1)S(1)} %constant_dynamic-update-slice_fusion, bf16[2048,768]{1,0:T(8,128)(2,1)} %all-gather.4.cloned.1.call-done), kind=kOutput, calls=%fused_computation.131 | convolution fusion | flops 3019898880 | bytes 12484608 | tf_op jit(solution)/shard_map/de,td->et/dot_general | solution.py:297
  52.4 35.3 %attend.1 = (bf16[4,192,512]{2,1,0:T(8,128)(2,1)S(1)}, f32[3,2048]{1,0:T(4,128)S(1)}) custom-call(s32[8]{0:T(128)S(1)} %get-tuple-element.96.low_ref, s32[8]{0:T(128)S(1)} %get-tuple-element.95.high_ref, s32[1,2048]{1,0:T(1,128)S(1)} %bitcast.128, s32[2048,1]{1,0:T(8,128)S(1)} %copy-done.3, bf16[192,2048]{1,0:T(8,128)(2,1)S(1)} %get-tuple-element.62.q_ref, ...), custom_call_target="tpu_custom_call" | custom-call | flops 3221225472 | bytes 3932160 | tf_op jit(solution)/shard_map/attend/pallas_call | solution.py:189
  87.8 2.4 constant_dynamic-update-slice_fusion.8
  90.2 1.8 constant_dynamic-update-slice_fusion.16
  92.0 3.7 %all-to-all-start = ((bf16[4,192,512]{2,1,0:T(8,128)(2,1)}), bf16[4,192,512]{2,1,0:T(8,128)(2,1)S(1)}, u32[]{:S(2)}, u32[]{:S(2)}) async-start(bf16[4,192,512]{2,1,0:T(8,128)(2,1)} %copy-done.7), calls=%async_computation | async-start | bytes 1572864 | tf_op jit(solution)/shard_map/all_to_all | solution.py:317
  96.3 1.8 constant_dynamic-update-slice_fusion.15
  98.1 1.9 constant_dynamic-update-slice_fusion.11
  100.1 1.8 constant_dynamic-update-slice_fusion.7
  103.4 1.8 constant_dynamic-update-slice_fusion.10
  105.2 1.9 constant_dynamic-update-slice_fusion.6
  108.8 2.6 convolution_bitcast_fusion
  111.5 2.9 fusion.22
  115.1 1.4 copy-done.41
  118.2 3.5 fusion.6
  126.0 1.8 slice.139
  127.8 1.4 copy-done.16
  130.5 3.0 multiply_reduce_fusion.2
  134.8 1.7 convolution_convert_fusion.6
  136.5 3.5 %all-to-all-start.1 = ((bf16[4,192,512]{2,1,0:T(8,128)(2,1)}), bf16[4,192,512]{2,1,0:T(8,128)(2,1)S(1)}, u32[]{:S(2)}, u32[]{:S(2)}) async-start(bf16[4,192,512]{2,1,0:T(8,128)(2,1)} %bitcast.146), calls=%async_computation.1 | async-start | bytes 1572864 | tf_op jit(solution)/shard_map/all_to_all | solution.py:335
  140.3 2.4 convolution_convert_fusion.4
  143.9 4.6 %add_convert_fusion = bf16[2,3,288,768]{3,2,0,1:T(8,128)(2,1)} fusion(bf16[2,3,288,768]{3,2,0,1:T(8,128)(2,1)} %collective-permute-done.9, bf16[4,3,288,768]{3,2,0,1:T(8,128)(2,1)} %copy-done.16), kind=kLoop, calls=%fused_computation.2 | loop fusion | flops 5308416 | bytes 7962624 | tf_op jit(solution)/shard_map/convert_element_type | solution.py:346
  148.5 3.1 all-to-all-done.1.g_ref
  151.7 2.7 slice_bitcast_fusion.1
  162.1 35.2 %attend_back.1 = (f32[192,2048]{1,0:T(8,128)S(1)}, f32[192,2048]{1,0:T(8,128)S(1)}, f32[192,2048]{1,0:T(8,128)S(1)}) custom-call(s32[8]{0:T(128)S(1)} %get-tuple-element.96.low_ref, s32[8]{0:T(128)S(1)} %get-tuple-element.95.high_ref, s32[1,2048]{1,0:T(1,128)S(1)} %bitcast.129, s32[2048,1]{1,0:T(8,128)S(1)} %copy-done.4, bf16[192,2048]{1,0:T(8,128)(2,1)S(1)} %copy-done.6, ...), custom_call_target="tpu_custom_call" | custom-call | flops 8053063680 | bytes 9437184 | tf_op jit(solution)/shard_map/attend_back/pallas_call | solution.py:235
  197.3 3.7 %fusion = bf16[3,288,768]{2,1,0:T(8,128)(2,1)} fusion(bf16[3,288,768]{2,1,0:T(8,128)(2,1)} %collective-permute-done.10, bf16[2,3,288,768]{3,2,0,1:T(8,128)(2,1)S(1)} %copy-done.19), kind=kLoop, calls=%fused_computation.10 | loop fusion | flops 2654208 | bytes 3981312 | tf_op jit(solution)/shard_map/convert_element_type | solution.py:351
  201.0 3.0 maximum_maximum_fusion
  204.0 5.7 %all-to-all-start.3 = ((bf16[8,144,768]{2,1,0:T(8,128)(2,1)}), bf16[8,144,768]{2,1,0:T(8,128)(2,1)}, u32[]{:S(2)}, u32[]{:S(2)}) async-start(bf16[8,144,768]{2,1,0:T(8,128)(2,1)} %bitcast.132), calls=%async_computation.4 | async-start | bytes 3538944 | tf_op jit(solution)/shard_map/all_to_all | solution.py:267
  210.8 2.3 add_convert_fusion.2
  213.3 2.0 copy-done.46
  215.2 2.0 convolution_convert_fusion.5
  218.6 32.3 %all-to-all-done.3 = bf16[8,144,768]{2,1,0:T(8,128)(2,1)} async-done(((bf16[8,144,768]{2,1,0:T(8,128)(2,1)}), bf16[8,144,768]{2,1,0:T(8,128)(2,1)}, u32[]{:S(2)}, u32[]{:S(2)}) %all-to-all-start.3) | async-done | bytes 1769504 | tf_op jit(solution)/shard_map/all_to_all | solution.py:267
  250.9 3.6 %all-to-all-start.2 = ((bf16[8,96,576]{2,1,0:T(8,128)(2,1)}), bf16[8,96,576]{2,1,0:T(8,128)(2,1)S(1)}, u32[]{:S(2)}, u32[]{:S(2)}) async-start(bf16[8,96,576]{2,1,0:T(8,128)(2,1)} %bitcast.35), calls=%async_computation.2 | async-start | bytes 1966080 | tf_op jit(solution)/shard_map/all_to_all | solution.py:267
  254.6 4.0 %convolution_convert_fusion.3 = bf16[2048,768]{1,0:T(8,128)(2,1)S(1)} fusion(bf16[192,2048]{1,0:T(8,128)(2,1)} %copy-done.40, bf16[192,2048]{1,0:T(8,128)(2,1)S(1)} %bitcast.148, bf16[192,2048]{1,0:T(8,128)(2,1)} %bitcast.150, bf16[768,192]{0,1:T(8,128)(2,1)S(1)} %copy-done.35, bf16[768,192]{0,1:T(8,128)(2,1)S(1)} %copy-done.33, ...), kind=kOutput, calls=%fused_computation.7 | convolution fusion | flops 1823244288 | bytes 6389760 | tf_op jit(solution)/shard_map/et,de->td/dot_general | solution.py:366
  258.7 1.6 copy-done.22
  261.5 2.6 reduce_sum.145
  264.2 4.2 %convolution_add_fusion.2 = f32[512,768]{1,0:T(8,128)} fusion(f32[512,768]{1,0:T(8,128)S(1)} %copy-done.15, bf16[512,1152]{1,0:T(8,128)(2,1)} %copy-done.48, bf16[1152,768]{1,0:T(8,128)(2,1)} %copy-done.43), kind=kOutput, calls=%fused_computation.55 | convolution fusion | flops 906362880 | bytes 6094848 | tf_op jit(solution)/shard_map/tf,fd->td/dot_general | solution.py:325
  268.7 2.4 fusion.12
  271.2 1.5 collective-permute-start.13
  272.6 10.6 %all-to-all-done.2 = bf16[8,96,576]{2,1,0:T(8,128)(2,1)S(1)} async-done(((bf16[8,96,576]{2,1,0:T(8,128)(2,1)}), bf16[8,96,576]{2,1,0:T(8,128)(2,1)S(1)}, u32[]{:S(2)}, u32[]{:S(2)}) %all-to-all-start.2) | async-done | bytes 884768 | tf_op jit(solution)/shard_map/all_to_all | solution.py:267
  283.4 35.4 %all_gather.14 = bf16[768,576]{1,0:T(8,128)(2,1)S(1)} all-gather(bf16[96,576]{1,0:T(8,128)(2,1)S(1)} %reduce_sum.143), channel_id=1, replica_groups=mesh['dp'=8,'tensor'=4] {'dp'}, dimensions={0}, use_global_device_ids=true | all-gather | bytes 995328 | tf_op jit(solution)/shard_map/all_gather | solution.py:269
  320.8 6.3 %psum.7 = f32[768]{0:T(1024)} all-reduce(f32[768]{0:T(1024)S(1)} %div.70), channel_id=1, replica_groups=mesh['dp'=8,'tensor'=4] {'tensor'}, use_global_device_ids=true, to_apply=%region_13.14 | all-reduce | flops 768 | bytes 6144 | tf_op jit(solution)/shard_map/psum | solution.py:384
  330.1 1.9 fusion.19
  332.0 3.0 multiply_add_fusion
  335.0 1.7 convert_element_type.178
  (199 shorter events, 47.2 us)
Async XLA Ops:
  7.2 2.2 copy-start.44
  7.2 34.8 %all-gather.4.cloned.1.call-start = ((), (), s32[]{:S(2)}) async-start(), calls=%async_computation.5 | async-start | bytes 3932160 | tf_op jit(solution)/shard_map/all_gather | solution.py:282
  9.4 4.8 %copy-start.24 = (bf16[3,768,192]{1,2,0:T(8,128)(2,1)S(1)}, bf16[3,768,192]{1,2,0:T(8,128)(2,1)}, u32[]{:S(2)}) copy-start(bf16[3,768,192]{1,2,0:T(8,128)(2,1)} %param.13) | copy-start | bytes 2654212
  10.6 100.9 %all-gather.6.cloned.1.call-start = ((), (), s32[]{:S(2)}) async-start(), calls=%async_computation.6 | async-start | bytes 1474560 | tf_op jit(solution)/shard_map/all_gather | solution.py:309
  18.4 31.1 %copy-start.25 = (f32[32,2048]{1,0:T(8,128)}, f32[32,2048]{1,0:T(8,128)S(1)}, u32[]{:S(2)}) copy-start(f32[32,2048]{1,0:T(8,128)S(1)} %get-tuple-element.90) | copy-start | bytes 786436
  18.4 31.1 %copy-start.27 = (f32[32,2048]{1,0:T(8,128)}, f32[32,2048]{1,0:T(8,128)S(1)}, u32[]{:S(2)}) copy-start(f32[32,2048]{1,0:T(8,128)S(1)} %get-tuple-element.91) | copy-start | bytes 786436
  42.0 50.0 %collective-permute-start.2 = (bf16[288,768]{1,0:T(8,128)(2,1)}, bf16[288,768]{1,0:T(8,128)(2,1)}, u32[]{:S(2)}, u32[]{:S(2)}) collective-permute-start(bf16[288,768]{1,0:T(8,128)(2,1)} %param.16), channel_id=1, source_target_pairs={{0,2},{1,3},{2,0},{3,1},{4,6},{5,7},{6,4},{7,5},{8,10},{9,11},{10,... | collective-permute-start | bytes 1327112 | tf_op jit(solution)/shard_map/ppermute | solution.py:262
  42.3 59.6 %collective-permute-start.7 = (bf16[288,768]{1,0:T(8,128)(2,1)}, bf16[288,768]{1,0:T(8,128)(2,1)}, u32[]{:S(2)}, u32[]{:S(2)}) collective-permute-start(bf16[288,768]{1,0:T(8,128)(2,1)} %param.16), channel_id=1, source_target_pairs={{0,1},{1,0},{2,3},{3,2},{4,5},{5,4},{6,7},{7,6},{8,9},{9,8},{10,11... | collective-permute-start | bytes 1327112 | tf_op jit(solution)/shard_map/ppermute | solution.py:262
  42.3 49.7 %collective-permute-start.1 = (bf16[288,768]{1,0:T(8,128)(2,1)}, bf16[288,768]{1,0:T(8,128)(2,1)}, u32[]{:S(2)}, u32[]{:S(2)}) collective-permute-start(bf16[288,768]{1,0:T(8,128)(2,1)} %get-tuple-element.30), channel_id=1, source_target_pairs={{0,2},{1,3},{2,0},{3,1},{4,6},{5,7},{6,4},{7,5},{8,10},{9,11},{10,... | collective-permute-start | bytes 1327112 | tf_op jit(solution)/shard_map/ppermute | solution.py:262
  44.0 59.3 %collective-permute-start.5 = (bf16[288,768]{1,0:T(8,128)(2,1)}, bf16[288,768]{1,0:T(8,128)(2,1)}, u32[]{:S(2)}, u32[]{:S(2)}) collective-permute-start(bf16[288,768]{1,0:T(8,128)(2,1)} %get-tuple-element.30), channel_id=1, source_target_pairs={{0,1},{1,0},{2,3},{3,2},{4,5},{5,4},{6,7},{7,6},{8,9},{9,8},{10,11... | collective-permute-start | bytes 1327112 | tf_op jit(solution)/shard_map/ppermute | solution.py:262
  50.3 37.5 %copy-start.5 = (bf16[192,2048]{1,0:T(8,128)(2,1)}, bf16[192,2048]{1,0:T(8,128)(2,1)S(1)}, u32[]{:S(2)}) copy-start(bf16[192,2048]{1,0:T(8,128)(2,1)S(1)} %get-tuple-element.62.q_ref) | copy-start | bytes 2359300
  50.8 41.2 %collective-permute-start = (bf16[288,768]{1,0:T(8,128)(2,1)}, bf16[288,768]{1,0:T(8,128)(2,1)}, u32[]{:S(2)}, u32[]{:S(2)}) collective-permute-start(bf16[288,768]{1,0:T(8,128)(2,1)} %get-tuple-element.29), channel_id=1, source_target_pairs={{0,2},{1,3},{2,0},{3,1},{4,6},{5,7},{6,4},{7,5},{8,10},{9,11},{10,... | collective-permute-start | bytes 1327112 | tf_op jit(solution)/shard_map/ppermute | solution.py:262
  87.8 4.2 %copy-start.7 = (bf16[4,192,512]{2,1,0:T(8,128)(2,1)}, bf16[4,192,512]{2,1,0:T(8,128)(2,1)S(1)}, u32[]{:S(2)}) copy-start(bf16[4,192,512]{2,1,0:T(8,128)(2,1)S(1)} %get-tuple-element.32.o_ref) | copy-start | bytes 2359300
  92.0 13.2 %collective-permute-start.3 = (bf16[288,768]{1,0:T(8,128)(2,1)}, bf16[288,768]{1,0:T(8,128)(2,1)}, u32[]{:S(2)}, u32[]{:S(2)}) collective-permute-start(bf16[288,768]{1,0:T(8,128)(2,1)} %get-tuple-element.29), channel_id=1, source_target_pairs={{0,1},{1,0},{2,3},{3,2},{4,5},{5,4},{6,7},{7,6},{8,9},{9,8},{10,11... | collective-permute-start | bytes 1327112 | tf_op jit(solution)/shard_map/ppermute | solution.py:262
  92.0 19.5 %all-to-all-start = ((bf16[4,192,512]{2,1,0:T(8,128)(2,1)}), bf16[4,192,512]{2,1,0:T(8,128)(2,1)S(1)}, u32[]{:S(2)}, u32[]{:S(2)}) async-start(bf16[4,192,512]{2,1,0:T(8,128)(2,1)} %copy-done.7), calls=%async_computation | async-start | bytes 1572864 | tf_op jit(solution)/shard_map/all_to_all | solution.py:317
  95.7 11.4 %collective-permute-start.8 = (bf16[288,768]{1,0:T(8,128)(2,1)}, bf16[288,768]{1,0:T(8,128)(2,1)S(1)}, u32[]{:S(2)}, u32[]{:S(2)}) collective-permute-start(bf16[288,768]{1,0:T(8,128)(2,1)} %collective-permute-done.2), channel_id=1, source_target_pairs={{0,1},{1,0},{2,3},{3,2},{4,5},{5,4},{6,7},{7,6},{8,9},{9,8},{10,11... | collective-permute-start | bytes 1327112 | tf_op jit(solution)/shard_map/ppermute | solution.py:262
  96.2 10.9 %collective-permute-start.6 = (bf16[288,768]{1,0:T(8,128)(2,1)}, bf16[288,768]{1,0:T(8,128)(2,1)S(1)}, u32[]{:S(2)}, u32[]{:S(2)}) collective-permute-start(bf16[288,768]{1,0:T(8,128)(2,1)} %collective-permute-done.1), channel_id=1, source_target_pairs={{0,1},{1,0},{2,3},{3,2},{4,5},{5,4},{6,7},{7,6},{8,9},{9,8},{10,11... | collective-permute-start | bytes 1327112 | tf_op jit(solution)/shard_map/ppermute | solution.py:262
  98.1 4.2 %copy-start.42 = (bf16[1152,768]{1,0:T(8,128)(2,1)S(1)}, bf16[1152,768]{1,0:T(8,128)(2,1)}, u32[]{:S(2)}) copy-start(bf16[1152,768]{1,0:T(8,128)(2,1)} %constant_dynamic-update-slice_fusion.15) | copy-start | bytes 5308420
  101.9 6.2 %collective-permute-start.4 = (bf16[288,768]{1,0:T(8,128)(2,1)}, bf16[288,768]{1,0:T(8,128)(2,1)S(1)}, u32[]{:S(2)}, u32[]{:S(2)}) collective-permute-start(bf16[288,768]{1,0:T(8,128)(2,1)} %collective-permute-done), channel_id=1, source_target_pairs={{0,1},{1,0},{2,3},{3,2},{4,5},{5,4},{6,7},{7,6},{8,9},{9,8},{10,11... | collective-permute-start | bytes 1327112 | tf_op jit(solution)/shard_map/ppermute | solution.py:262
  105.2 3.7 %copy-start.29 = (f32[512,768]{1,0:T(8,128)S(1)}, f32[512,768]{1,0:T(8,128)}, u32[]{:S(2)}) copy-start(f32[512,768]{1,0:T(8,128)} %param.17) | copy-start | bytes 4718596
  111.5 3.0 copy-start.20
  111.5 3.3 copy-start.45
  114.5 19.1 %copy-start.14 = (f32[512,768]{1,0:T(8,128)}, f32[512,768]{1,0:T(8,128)S(1)}, u32[]{:S(2)}) copy-start(f32[512,768]{1,0:T(8,128)S(1)} %get-tuple-element.93) | copy-start | bytes 4718596
  121.7 2.3 copy-start.48
  126.0 3.2 copy-start.16
  129.2 14.7 %collective-permute-start.9 = (bf16[2,3,288,768]{3,2,0,1:T(8,128)(2,1)}, bf16[2,3,288,768]{3,2,0,1:T(8,128)(2,1)}, u32[]{:S(2)}, u32[]{:S(2)}) collective-permute-start(bf16[2,3,288,768]{3,2,0,1:T(8,128)(2,1)} %slice.139), channel_id=1, source_target_pairs={{0,1},{1,0},{2,3},{3,2},{4,5},{5,4},{6,7},{7,6},{8,9},{9,8},{10,11... | collective-permute-start | bytes 7962632 | tf_op jit(solution)/shard_map/ppermute | solution.py:262
  136.5 15.1 %all-to-all-start.1 = ((bf16[4,192,512]{2,1,0:T(8,128)(2,1)}), bf16[4,192,512]{2,1,0:T(8,128)(2,1)S(1)}, u32[]{:S(2)}, u32[]{:S(2)}) async-start(bf16[4,192,512]{2,1,0:T(8,128)(2,1)} %bitcast.146), calls=%async_computation.1 | async-start | bytes 1572864 | tf_op jit(solution)/shard_map/all_to_all | solution.py:335
  140.0 61.0 %reduce-scatter.2.cloned.1.call-start = ((), (), s32[]{:S(2)}) async-start(), calls=%async_computation.7 | async-start | bytes 1597440 | tf_op jit(solution)/shard_map/reduce_scatter | solution.py:352
  151.6 2.8 copy-start.9
  154.4 42.9 %collective-permute-start.10 = (bf16[3,288,768]{2,1,0:T(8,128)(2,1)}, bf16[3,288,768]{2,1,0:T(8,128)(2,1)}, u32[]{:S(2)}, u32[]{:S(2)}) collective-permute-start(bf16[3,288,768]{2,1,0:T(8,128)(2,1)} %slice_bitcast_fusion.1), channel_id=1, source_target_pairs={{0,2},{1,3},{2,0},{3,1},{4,6},{5,7},{6,4},{7,5},{8,10},{9,11},{10,... | collective-permute-start | bytes 3981320 | tf_op jit(solution)/shard_map/ppermute | solution.py:262
  162.1 35.2 %copy-start.19 = (bf16[2,3,288,768]{3,2,0,1:T(8,128)(2,1)S(1)}, bf16[2,3,288,768]{3,2,0,1:T(8,128)(2,1)}, u32[]{:S(2)}) copy-start(bf16[2,3,288,768]{3,2,0,1:T(8,128)(2,1)} %add_convert_fusion) | copy-start | bytes 7962628
  197.3 3.7 %copy-start = (f32[192,2048]{1,0:T(8,128)}, f32[192,2048]{1,0:T(8,128)S(1)}, u32[]{:S(2)}) copy-start(f32[192,2048]{1,0:T(8,128)S(1)} %get-tuple-element.43) | copy-start | bytes 4718596
  197.3 3.7 %copy-start.1 = (f32[192,2048]{1,0:T(8,128)}, f32[192,2048]{1,0:T(8,128)S(1)}, u32[]{:S(2)}) copy-start(f32[192,2048]{1,0:T(8,128)S(1)} %get-tuple-element.44) | copy-start | bytes 4718596
  204.0 46.9 %all-to-all-start.3 = ((bf16[8,144,768]{2,1,0:T(8,128)(2,1)}), bf16[8,144,768]{2,1,0:T(8,128)(2,1)}, u32[]{:S(2)}, u32[]{:S(2)}) async-start(bf16[8,144,768]{2,1,0:T(8,128)(2,1)} %bitcast.132), calls=%async_computation.4 | async-start | bytes 3538944 | tf_op jit(solution)/shard_map/all_to_all | solution.py:267
  209.9 3.4 copy-start.40
  213.2 4.0 %copy-start.39 = (bf16[3,2,32,2048]{3,2,1,0:T(8,128)(2,1)}, bf16[3,2,32,2048]{3,2,1,0:T(8,128)(2,1)S(1)}, u32[]{:S(2)}) copy-start(bf16[3,2,32,2048]{3,2,1,0:T(8,128)(2,1)S(1)} %pad_maximum_fusion.8) | copy-start | bytes 2359300
  217.3 37.3 %copy-start.31 = (bf16[768,192]{0,1:T(8,128)(2,1)S(1)}, bf16[768,192]{0,1:T(8,128)(2,1)}, u32[]{:S(2)}) copy-start(bf16[768,192]{0,1:T(8,128)(2,1)} %get-tuple-element.77) | copy-start | bytes 884740
  217.3 37.3 %copy-start.33 = (bf16[768,192]{0,1:T(8,128)(2,1)S(1)}, bf16[768,192]{0,1:T(8,128)(2,1)}, u32[]{:S(2)}) copy-start(bf16[768,192]{0,1:T(8,128)(2,1)} %get-tuple-element.78) | copy-start | bytes 884740
  217.3 37.3 %copy-start.35 = (bf16[768,192]{0,1:T(8,128)(2,1)S(1)}, bf16[768,192]{0,1:T(8,128)(2,1)}, u32[]{:S(2)}) copy-start(bf16[768,192]{0,1:T(8,128)(2,1)} %get-tuple-element.80) | copy-start | bytes 884740
  250.9 32.3 %all-to-all-start.2 = ((bf16[8,96,576]{2,1,0:T(8,128)(2,1)}), bf16[8,96,576]{2,1,0:T(8,128)(2,1)S(1)}, u32[]{:S(2)}, u32[]{:S(2)}) async-start(bf16[8,96,576]{2,1,0:T(8,128)(2,1)} %bitcast.35), calls=%async_computation.2 | async-start | bytes 1966080 | tf_op jit(solution)/shard_map/all_to_all | solution.py:267
  254.5 80.5 %all-gather.8.cloned.1.call-start = ((), (), s32[]{:S(2)}) async-start(), calls=%async_computation.8 | async-start | bytes 1990656 | tf_op jit(solution)/shard_map/all_gather | solution.py:269
  261.5 2.6 copy-start.15
  261.5 7.2 %collective-permute-start.12 = (bf16[512,768]{1,0:T(8,128)(2,1)}, bf16[512,768]{1,0:T(8,128)(2,1)}, u32[]{:S(2)}, u32[]{:S(2)}) collective-permute-start(bf16[512,768]{1,0:T(8,128)(2,1)} %get-tuple-element.69), channel_id=1, source_target_pairs={{0,1},{1,0},{2,3},{3,2},{4,5},{5,4},{6,7},{7,6},{8,9},{9,8},{10,11... | collective-permute-start | bytes 2359304 | tf_op jit(solution)/shard_map/ppermute | solution.py:262
  268.3 60.2 %collective-permute-start.11 = (bf16[512,768]{1,0:T(8,128)(2,1)}, bf16[512,768]{1,0:T(8,128)(2,1)S(1)}, u32[]{:S(2)}, u32[]{:S(2)}) collective-permute-start(bf16[512,768]{1,0:T(8,128)(2,1)} %get-tuple-element.68), channel_id=1, source_target_pairs={{0,1},{1,0},{2,3},{3,2},{4,5},{5,4},{6,7},{7,6},{8,9},{9,8},{10,11... | collective-permute-start | bytes 2359304 | tf_op jit(solution)/shard_map/ppermute | solution.py:262
  271.2 57.4 %collective-permute-start.13 = (bf16[512,768]{1,0:T(8,128)(2,1)}, bf16[512,768]{1,0:T(8,128)(2,1)}, u32[]{:S(2)}, u32[]{:S(2)}) collective-permute-start(bf16[512,768]{1,0:T(8,128)(2,1)} %fusion.12), channel_id=1, source_target_pairs={{0,2},{1,3},{2,0},{3,1},{4,6},{5,7},{6,4},{7,5},{8,10},{9,11},{10,... | collective-permute-start | bytes 2359304 | tf_op jit(solution)/shard_map/ppermute | solution.py:262
  327.1 2.5 copy-start.23
  327.2 2.9 copy-start.13
  328.5 3.5 copy-start.18
  (23 other events, 32.3 us)
Sparse Core Ops, SparseCore 0:
  10.7 31.2 all-gather.3
  51.3 25.0 all-gather.5
  151.8 33.5 reduce-scatter.1
  264.3 58.9 all-gather.7

commit v3 on v2

--- a/solution.py
+++ b/solution.py
@@ -262,11 +262,14 @@
     return lax.ppermute(values, "tensor", [(i, i ^ distance) for i in range(parts)])
 
 
-def sum_groups(values, groups):
+def share_of(values, groups):
     rows, columns = values.shape
     received = lax.all_to_all(values.reshape(groups, rows // groups, columns), "dp", 0, 0)
-    share = jnp.sum(received.astype(jnp.float32), axis=0).astype(jnp.bfloat16)
-    return lax.all_gather(share, "dp", axis=0, tiled=True)
+    return jnp.sum(received.astype(jnp.float32), axis=0).astype(jnp.bfloat16)
+
+
+def sum_groups(values, groups):
+    return lax.all_gather(share_of(values, groups), "dp", axis=0, tiled=True)
 
 
 def shards(tokens, seq_ids, gain_attn, gain_mlp, w_qkv, w_out, w_gu, w_down, cotangent):
@@ -374,12 +377,14 @@
     grad_normed_one = mine_two + swap(across_two, 2, parts).astype(f32)
     grad_qkv = dot("td,et->de", normed_all, grad_proj_t)
     groups = lax.axis_size("dp")
-    grad_qkv = sum_groups(grad_qkv.astype(bf16), groups).astype(f32)
+    qkv_share = share_of(grad_qkv.astype(bf16), groups)
     count = 3 * hidden + width + 16
     padding = -count % (16 * groups)
     mine = jnp.concatenate(
         [mlp_mine.reshape(3 * hidden, model), out_mine, jnp.zeros((padding, model), bf16)]
     )
+    mine, qkv_share = lax.optimization_barrier((mine, qkv_share))
+    grad_qkv = lax.all_gather(qkv_share, "dp", axis=0, tiled=True).astype(f32)
     summed = sum_groups(mine, groups)
     gain_one = lax.psum(jnp.sum(grad_qkv * w_flat.astype(f32), axis=1) / gain_attn, "tensor")
     grad_qkv = jnp.stack([grad_qkv[:, i * width : (i + 1) * width] for i in range(3)])

time: 353 us -> 360 us (1.020); the launches traced: 348 us -> 362 us
  waiting for transfers between devices: 69.7 us -> 82.9 us
  starting transfers between devices: 22.9 us -> 29.8 us
  other arithmetic: 38.6 us -> 33.6 us
    all_to_all x2, waiting for transfers between devices: 42.9 us -> 56.2 us  [share_of(): lax.all_to_all(values.reshape(groups, rows // groups, columns), 'dp', 0, 0)]
    all_to_all x2, starting transfers between devices: 9.37 us -> 15.3 us  [share_of(): lax.all_to_all(values.reshape(groups, rows // groups, columns), 'dp', 0, 0)]
    unnamed x111 -> x103, local copies, waits for them, and re-layouts: 36.4 us -> 33.5 us
  transfers between devices with their start and end apart: 22 -> 22, of which waited for: 4 -> 4; matrix products, arithmetic and copies ran while one was open for 24% -> 21% of each run, Pallas kernels for 20% -> 20%
where the time goes in v3:
time: 360 us; the launch traced here: 362 us
  waiting for transfers between devices  82.9 us (23%)
  Pallas kernels  71.6 us (20%)
  local copies, waits for them, and re-layouts  49.6 us (14%)
  blocking collectives  41.7 us (12%)
  matrix products  38.3 us (11%)
  other arithmetic  33.6 us (9%)
  starting transfers between devices  29.8 us (8%)
  between operations  14.6 us (4%)
    all_to_all x2, waiting for transfers between devices, share_of(): lax.all_to_all(values.reshape(groups, rows // groups, columns), 'dp', 0, 0)  56.2 us
    pallas_call x1, Pallas kernels, attend_back(): pl.pallas_call(functools.partial(backward_kernel, heads), grid_spec=grid_...  36.3 us
    pallas_call x1, Pallas kernels, attend(): pl.pallas_call(functools.partial(forward_kernel, heads), grid_spec=grid_s...  35.3 us
    all_gather x1, blocking collectives, shards(): grad_qkv = lax.all_gather(qkv_share, 'dp', axis=0, tiled=True).astype(f32)  35.1 us
    unnamed x103, local copies, waits for them, and re-layouts  33.5 us
    all_gather x1, waiting for transfers between devices, shards(): lax.all_gather(normed_one.astype(bf16), 'tensor', axis=0, tiled=True)  23.3 us
    all_to_all x2, starting transfers between devices, share_of(): lax.all_to_all(values.reshape(groups, rows // groups, columns), 'dp', 0, 0)  15.3 us
  transfers between devices with their start and end apart: 22, of which 4 were waited for; matrix products, arithmetic and copies ran while one was open for 21% of the time, Pallas kernels for 20%

profile of v3, /device:TPU:0, one launch (start us, length us, event | category | flops | bytes accessed | tf_op | source)
XLA Modules:
  0.0 362.2 jit_solution(4524748338506350203)
XLA Ops:
  7.2 1.7 reduce_sum.134
  10.7 1.8 convert_reduce_fusion
  12.6 1.4 copy.66.idc_ref
  18.6 23.3 %all-gather.4.cloned.1.call-done = bf16[2048,768]{1,0:T(8,128)(2,1)} async-done(((bf16[512,768]{1,0:T(8,128)(2,1)}), bf16[2048,768]{1,0:T(8,128)(2,1)}) %all-gather.4.cloned.1.call-update) | async-done | bytes 3145744 | tf_op jit(solution)/shard_map/all_gather | solution.py:285
  42.3 1.7 collective-permute-start.1
  44.2 5.6 %fusion.23 = f32[960,2048]{1,0:T(8,128)S(1)} fusion(bf16[768,960]{0,1:T(8,128)(2,1)} %copy-done.40, bf16[2048,768]{1,0:T(8,128)(2,1)} %all-gather.4.cloned.1.call-done), kind=kOutput, calls=%fused_computation.131 | convolution fusion | flops 3019898880 | bytes 12484608 | tf_op jit(solution)/shard_map/de,td->et/dot_general | solution.py:300
  52.9 35.3 %attend.1 = (bf16[4,192,512]{2,1,0:T(8,128)(2,1)S(1)}, f32[3,2048]{1,0:T(4,128)S(1)}) custom-call(s32[8]{0:T(128)S(1)} %get-tuple-element.100.low_ref, s32[8]{0:T(128)S(1)} %get-tuple-element.99.high_ref, s32[1,2048]{1,0:T(1,128)S(1)} %bitcast.128, s32[2048,1]{1,0:T(8,128)S(1)} %copy-done.1, bf16[192,2048]{1,0:T(8,128)(2,1)S(1)} %get-tuple-element.66.q_ref, ...), custom_call_target="tpu_custom_call" | custom-call | flops 3221225472 | bytes 3932160 | tf_op jit(solution)/shard_map/attend/pallas_call | solution.py:189
  88.2 2.4 constant_dynamic-update-slice_fusion.8
  90.6 1.8 constant_dynamic-update-slice_fusion.16
  92.5 4.4 %all-to-all-start = ((bf16[4,192,512]{2,1,0:T(8,128)(2,1)}), bf16[4,192,512]{2,1,0:T(8,128)(2,1)}, u32[]{:S(2)}, u32[]{:S(2)}) async-start(bf16[4,192,512]{2,1,0:T(8,128)(2,1)} %copy-done.3), calls=%async_computation | async-start | bytes 1572864 | tf_op jit(solution)/shard_map/all_to_all | solution.py:320
  97.5 1.8 constant_dynamic-update-slice_fusion.15
  99.3 1.9 constant_dynamic-update-slice_fusion.11
  101.2 1.8 constant_dynamic-update-slice_fusion.7
  104.5 1.8 constant_dynamic-update-slice_fusion.10
  106.3 1.9 constant_dynamic-update-slice_fusion.6
  110.0 2.7 convolution_bitcast_fusion
  112.6 2.9 fusion.22
  116.2 1.4 copy-done.36
  119.3 3.6 fusion.6
  127.3 1.8 slice.139
  129.1 1.4 copy-done.10
  131.7 3.1 multiply_reduce_fusion.2
  136.2 1.7 convolution_convert_fusion.6
  137.9 4.2 %all-to-all-start.1 = ((bf16[4,192,512]{2,1,0:T(8,128)(2,1)}), bf16[4,192,512]{2,1,0:T(8,128)(2,1)}, u32[]{:S(2)}, u32[]{:S(2)}) async-start(bf16[4,192,512]{2,1,0:T(8,128)(2,1)} %bitcast.148), calls=%async_computation.1 | async-start | bytes 1572864 | tf_op jit(solution)/shard_map/all_to_all | solution.py:338
  142.3 2.4 convolution_convert_fusion.4
  145.9 4.7 %add_convert_fusion = bf16[2,3,288,768]{3,2,0,1:T(8,128)(2,1)} fusion(bf16[2,3,288,768]{3,2,0,1:T(8,128)(2,1)} %collective-permute-done.9, bf16[4,3,288,768]{3,2,0,1:T(8,128)(2,1)} %copy-done.10), kind=kLoop, calls=%fused_computation.2 | loop fusion | flops 5308416 | bytes 7962624 | tf_op jit(solution)/shard_map/convert_element_type | solution.py:349
  150.6 3.2 all-to-all-done.1.g_ref
  153.8 2.5 slice_bitcast_fusion.1
  161.5 36.3 %attend_back.1 = (f32[192,2048]{1,0:T(8,128)S(1)}, f32[192,2048]{1,0:T(8,128)S(1)}, f32[192,2048]{1,0:T(8,128)S(1)}) custom-call(s32[8]{0:T(128)S(1)} %get-tuple-element.100.low_ref, s32[8]{0:T(128)S(1)} %get-tuple-element.99.high_ref, s32[1,2048]{1,0:T(1,128)S(1)} %bitcast.129, s32[2048,1]{1,0:T(8,128)S(1)} %copy-done.2, ...), custom_call_target="tpu_custom_call" | custom-call | flops 8053063680 | bytes 9437184 | tf_op jit(solution)/shard_map/attend_back/pallas_call | solution.py:235
  197.9 1.7 fusion
  203.6 2.0 convolution_convert_fusion.5
  206.9 11.6 %all-to-all-start.2 = ((bf16[8,96,576]{2,1,0:T(8,128)(2,1)}), bf16[8,96,576]{2,1,0:T(8,128)(2,1)S(1)}, u32[]{:S(2)}, u32[]{:S(2)}) async-start(bf16[8,96,576]{2,1,0:T(8,128)(2,1)} %bitcast.37), calls=%async_computation.3 | async-start | bytes 1966080 | tf_op jit(solution)/shard_map/all_to_all | solution.py:267
  218.5 2.5 maximum_maximum_fusion
  221.1 21.6 %all-to-all-done.2 = bf16[8,96,576]{2,1,0:T(8,128)(2,1)S(1)} async-done(((bf16[8,96,576]{2,1,0:T(8,128)(2,1)}), bf16[8,96,576]{2,1,0:T(8,128)(2,1)S(1)}, u32[]{:S(2)}, u32[]{:S(2)}) %all-to-all-start.2) | async-done | bytes 884768 | tf_op jit(solution)/shard_map/all_to_all | solution.py:267
  243.5 3.7 %all-to-all-start.3 = ((bf16[8,144,768]{2,1,0:T(8,128)(2,1)}), bf16[8,144,768]{2,1,0:T(8,128)(2,1)S(1)}, u32[]{:S(2)}, u32[]{:S(2)}) async-start(bf16[8,144,768]{2,1,0:T(8,128)(2,1)} %bitcast.130), calls=%async_computation.4 | async-start | bytes 3538944 | tf_op jit(solution)/shard_map/all_to_all | solution.py:267
  247.3 4.3 %convolution_convert_fusion.3 = bf16[2048,768]{1,0:T(8,128)(2,1)S(1)} fusion(bf16[192,2048]{1,0:T(8,128)(2,1)} %copy-done.34, bf16[192,2048]{1,0:T(8,128)(2,1)} %bitcast.145, bf16[192,2048]{1,0:T(8,128)(2,1)} %bitcast.147, bf16[768,192]{0,1:T(8,128)(2,1)S(1)} %copy-done.28, bf16[768,192]{0,1:T(8,128)(2,1)S(1)} %copy-done.26, bf16[768,192]{0,1:T(8,128)(2,1)S(1)} %copy-done.24), kind=kOutput, calls=%fused_computation.7 | convolution fusion | flops 1823244288 | bytes 6389760 | tf_op jit(solution)/shard_map/et,de->td/dot_general | solution.py:369
  251.6 1.4 dynamic-slice_bitcast_fusion.1
  253.7 34.7 %all-to-all-done.3 = bf16[8,144,768]{2,1,0:T(8,128)(2,1)S(1)} async-done(((bf16[8,144,768]{2,1,0:T(8,128)(2,1)}), bf16[8,144,768]{2,1,0:T(8,128)(2,1)S(1)}, u32[]{:S(2)}, u32[]{:S(2)}) %all-to-all-start.3) | async-done | bytes 1769504 | tf_op jit(solution)/shard_map/all_to_all | solution.py:267
  289.4 4.2 %convolution_add_fusion.2 = f32[512,768]{1,0:T(8,128)} fusion(f32[512,768]{1,0:T(8,128)S(1)} %copy-done.9, bf16[512,1152]{1,0:T(8,128)(2,1)} %copy-done.44, bf16[1152,768]{1,0:T(8,128)(2,1)} %copy-done.38), kind=kOutput, calls=%fused_computation.55 | convolution fusion | flops 906362880 | bytes 6094848 | tf_op jit(solution)/shard_map/tf,fd->td/dot_general | solution.py:328
  293.6 2.5 fusion.12
  296.1 1.4 collective-permute-start.13
  297.5 35.1 %all_gather.14 = bf16[768,576]{1,0:T(8,128)(2,1)S(1)} all-gather(bf16[96,576]{1,0:T(8,128)(2,1)S(1)} %copy-done.35), channel_id=1, replica_groups=mesh['dp'=8,'tensor'=4] {'dp'}, dimensions={0}, use_global_device_ids=true | all-gather | bytes 995328 | tf_op jit(solution)/shard_map/all_gather | solution.py:387
  334.6 6.7 %psum.7 = f32[768]{0:T(1024)} all-reduce(f32[768]{0:T(1024)S(1)} %div.70), channel_id=1, replica_groups=mesh['dp'=8,'tensor'=4] {'tensor'}, use_global_device_ids=true, to_apply=%region_14.15 | all-reduce | flops 768 | bytes 6144 | tf_op jit(solution)/shard_map/psum | solution.py:389
  341.4 1.3 pad_maximum_fusion.2
  344.3 1.9 fusion.19
  346.2 3.0 multiply_add_fusion
  349.2 1.7 convert_element_type.178
  351.7 1.3 pad_maximum_fusion.3
  (191 shorter events, 44.5 us)
Async XLA Ops:
  7.2 1.9 copy-start.6
  7.2 2.2 copy-start.39
  7.2 34.8 %all-gather.4.cloned.1.call-start = ((), (), s32[]{:S(2)}) async-start(), calls=%async_computation.5 | async-start | bytes 3932160 | tf_op jit(solution)/shard_map/all_gather | solution.py:285
  9.4 4.8 %copy-start.17 = (bf16[3,768,192]{1,2,0:T(8,128)(2,1)S(1)}, bf16[3,768,192]{1,2,0:T(8,128)(2,1)}, u32[]{:S(2)}) copy-start(bf16[3,768,192]{1,2,0:T(8,128)(2,1)} %param.13) | copy-start | bytes 2654212
  10.6 102.1 %all-gather.6.cloned.1.call-start = ((), (), s32[]{:S(2)}) async-start(), calls=%async_computation.6 | async-start | bytes 1474560 | tf_op jit(solution)/shard_map/all_gather | solution.py:312
  18.6 31.3 %copy-start.18 = (f32[32,2048]{1,0:T(8,128)}, f32[32,2048]{1,0:T(8,128)S(1)}, u32[]{:S(2)}) copy-start(f32[32,2048]{1,0:T(8,128)S(1)} %get-tuple-element.94) | copy-start | bytes 786436
  18.6 31.3 %copy-start.20 = (f32[32,2048]{1,0:T(8,128)}, f32[32,2048]{1,0:T(8,128)S(1)}, u32[]{:S(2)}) copy-start(f32[32,2048]{1,0:T(8,128)S(1)} %get-tuple-element.95) | copy-start | bytes 786436
  42.0 50.5 %collective-permute-start.2 = (bf16[288,768]{1,0:T(8,128)(2,1)}, bf16[288,768]{1,0:T(8,128)(2,1)}, u32[]{:S(2)}, u32[]{:S(2)}) collective-permute-start(bf16[288,768]{1,0:T(8,128)(2,1)} %param.16), channel_id=1, source_target_pairs={{0,2},{1,3},{2,0},{3,1},{4,6},{5,7},{6,4},{7,5},{8,10},{9,11},{10,... | collective-permute-start | bytes 1327112 | tf_op jit(solution)/shard_map/ppermute | solution.py:262
  42.3 60.7 %collective-permute-start.7 = (bf16[288,768]{1,0:T(8,128)(2,1)}, bf16[288,768]{1,0:T(8,128)(2,1)}, u32[]{:S(2)}, u32[]{:S(2)}) collective-permute-start(bf16[288,768]{1,0:T(8,128)(2,1)} %param.16), channel_id=1, source_target_pairs={{0,1},{1,0},{2,3},{3,2},{4,5},{5,4},{6,7},{7,6},{8,9},{9,8},{10,11... | collective-permute-start | bytes 1327112 | tf_op jit(solution)/shard_map/ppermute | solution.py:262
  42.3 50.2 %collective-permute-start.1 = (bf16[288,768]{1,0:T(8,128)(2,1)}, bf16[288,768]{1,0:T(8,128)(2,1)}, u32[]{:S(2)}, u32[]{:S(2)}) collective-permute-start(bf16[288,768]{1,0:T(8,128)(2,1)} %get-tuple-element.32), channel_id=1, source_target_pairs={{0,2},{1,3},{2,0},{3,1},{4,6},{5,7},{6,4},{7,5},{8,10},{9,11},{10,... | collective-permute-start | bytes 1327112 | tf_op jit(solution)/shard_map/ppermute | solution.py:262
  44.0 60.5 %collective-permute-start.5 = (bf16[288,768]{1,0:T(8,128)(2,1)}, bf16[288,768]{1,0:T(8,128)(2,1)}, u32[]{:S(2)}, u32[]{:S(2)}) collective-permute-start(bf16[288,768]{1,0:T(8,128)(2,1)} %get-tuple-element.32), channel_id=1, source_target_pairs={{0,1},{1,0},{2,3},{3,2},{4,5},{5,4},{6,7},{7,6},{8,9},{9,8},{10,11... | collective-permute-start | bytes 1327112 | tf_op jit(solution)/shard_map/ppermute | solution.py:262
  51.3 41.2 %collective-permute-start = (bf16[288,768]{1,0:T(8,128)(2,1)}, bf16[288,768]{1,0:T(8,128)(2,1)}, u32[]{:S(2)}, u32[]{:S(2)}) collective-permute-start(bf16[288,768]{1,0:T(8,128)(2,1)} %get-tuple-element.31), channel_id=1, source_target_pairs={{0,2},{1,3},{2,0},{3,1},{4,6},{5,7},{6,4},{7,5},{8,10},{9,11},{10,... | collective-permute-start | bytes 1327112 | tf_op jit(solution)/shard_map/ppermute | solution.py:262
  88.2 4.2 %copy-start.3 = (bf16[4,192,512]{2,1,0:T(8,128)(2,1)}, bf16[4,192,512]{2,1,0:T(8,128)(2,1)S(1)}, u32[]{:S(2)}) copy-start(bf16[4,192,512]{2,1,0:T(8,128)(2,1)S(1)} %get-tuple-element.34.o_ref) | copy-start | bytes 2359300
  92.4 13.9 %collective-permute-start.3 = (bf16[288,768]{1,0:T(8,128)(2,1)}, bf16[288,768]{1,0:T(8,128)(2,1)}, u32[]{:S(2)}, u32[]{:S(2)}) collective-permute-start(bf16[288,768]{1,0:T(8,128)(2,1)} %get-tuple-element.31), channel_id=1, source_target_pairs={{0,1},{1,0},{2,3},{3,2},{4,5},{5,4},{6,7},{7,6},{8,9},{9,8},{10,11... | collective-permute-start | bytes 1327112 | tf_op jit(solution)/shard_map/ppermute | solution.py:262
  92.5 20.2 %all-to-all-start = ((bf16[4,192,512]{2,1,0:T(8,128)(2,1)}), bf16[4,192,512]{2,1,0:T(8,128)(2,1)}, u32[]{:S(2)}, u32[]{:S(2)}) async-start(bf16[4,192,512]{2,1,0:T(8,128)(2,1)} %copy-done.3), calls=%async_computation | async-start | bytes 1572864 | tf_op jit(solution)/shard_map/all_to_all | solution.py:320
  96.9 11.4 %collective-permute-start.8 = (bf16[288,768]{1,0:T(8,128)(2,1)}, bf16[288,768]{1,0:T(8,128)(2,1)S(1)}, u32[]{:S(2)}, u32[]{:S(2)}) collective-permute-start(bf16[288,768]{1,0:T(8,128)(2,1)} %collective-permute-done.2), channel_id=1, source_target_pairs={{0,1},{1,0},{2,3},{3,2},{4,5},{5,4},{6,7},{7,6},{8,9},{9,8},{10,11... | collective-permute-start | bytes 1327112 | tf_op jit(solution)/shard_map/ppermute | solution.py:262
  97.4 10.9 %collective-permute-start.6 = (bf16[288,768]{1,0:T(8,128)(2,1)}, bf16[288,768]{1,0:T(8,128)(2,1)S(1)}, u32[]{:S(2)}, u32[]{:S(2)}) collective-permute-start(bf16[288,768]{1,0:T(8,128)(2,1)} %collective-permute-done.1), channel_id=1, source_target_pairs={{0,1},{1,0},{2,3},{3,2},{4,5},{5,4},{6,7},{7,6},{8,9},{9,8},{10,11... | collective-permute-start | bytes 1327112 | tf_op jit(solution)/shard_map/ppermute | solution.py:262
  99.3 4.2 %copy-start.37 = (bf16[1152,768]{1,0:T(8,128)(2,1)S(1)}, bf16[1152,768]{1,0:T(8,128)(2,1)}, u32[]{:S(2)}) copy-start(bf16[1152,768]{1,0:T(8,128)(2,1)} %constant_dynamic-update-slice_fusion.15) | copy-start | bytes 5308420
  103.0 6.2 %collective-permute-start.4 = (bf16[288,768]{1,0:T(8,128)(2,1)}, bf16[288,768]{1,0:T(8,128)(2,1)S(1)}, u32[]{:S(2)}, u32[]{:S(2)}) collective-permute-start(bf16[288,768]{1,0:T(8,128)(2,1)} %collective-permute-done), channel_id=1, source_target_pairs={{0,1},{1,0},{2,3},{3,2},{4,5},{5,4},{6,7},{7,6},{8,9},{9,8},{10,11... | collective-permute-start | bytes 1327112 | tf_op jit(solution)/shard_map/ppermute | solution.py:262
  106.3 3.7 %copy-start.22 = (f32[512,768]{1,0:T(8,128)S(1)}, f32[512,768]{1,0:T(8,128)}, u32[]{:S(2)}) copy-start(f32[512,768]{1,0:T(8,128)} %param.17) | copy-start | bytes 4718596
  108.3 1.7 copy-start.38
  112.6 3.3 copy-start.41
  115.6 19.3 %copy-start.8 = (f32[512,768]{1,0:T(8,128)}, f32[512,768]{1,0:T(8,128)S(1)}, u32[]{:S(2)}) copy-start(f32[512,768]{1,0:T(8,128)S(1)} %get-tuple-element.97) | copy-start | bytes 4718596
  115.6 2.0 copy-start.36
  122.9 2.3 copy-start.44
  127.3 3.2 copy-start.10
  130.4 15.5 %collective-permute-start.9 = (bf16[2,3,288,768]{3,2,0,1:T(8,128)(2,1)}, bf16[2,3,288,768]{3,2,0,1:T(8,128)(2,1)}, u32[]{:S(2)}, u32[]{:S(2)}) collective-permute-start(bf16[2,3,288,768]{3,2,0,1:T(8,128)(2,1)} %slice.139), channel_id=1, source_target_pairs={{0,1},{1,0},{2,3},{3,2},{4,5},{5,4},{6,7},{7,6},{8,9},{9,8},{10,11... | collective-permute-start | bytes 7962632 | tf_op jit(solution)/shard_map/ppermute | solution.py:262
  137.9 15.9 %all-to-all-start.1 = ((bf16[4,192,512]{2,1,0:T(8,128)(2,1)}), bf16[4,192,512]{2,1,0:T(8,128)(2,1)}, u32[]{:S(2)}, u32[]{:S(2)}) async-start(bf16[4,192,512]{2,1,0:T(8,128)(2,1)} %bitcast.148), calls=%async_computation.1 | async-start | bytes 1572864 | tf_op jit(solution)/shard_map/all_to_all | solution.py:338
  142.1 76.5 %reduce-scatter.2.cloned.1.call-start = ((), (), s32[]{:S(2)}) async-start(), calls=%async_computation.7 | async-start | bytes 1597440 | tf_op jit(solution)/shard_map/reduce_scatter | solution.py:355
  156.3 41.6 %collective-permute-start.10 = (bf16[3,288,768]{2,1,0:T(8,128)(2,1)}, bf16[3,288,768]{2,1,0:T(8,128)(2,1)}, u32[]{:S(2)}, u32[]{:S(2)}) collective-permute-start(bf16[3,288,768]{2,1,0:T(8,128)(2,1)} %slice_bitcast_fusion.1), channel_id=1, source_target_pairs={{0,2},{1,3},{2,0},{3,1},{4,6},{5,7},{6,4},{7,5},{8,10},{9,11},{10,... | collective-permute-start | bytes 3981320 | tf_op jit(solution)/shard_map/ppermute | solution.py:262
  161.5 36.4 %copy-start.13 = (bf16[2,3,288,768]{3,2,0,1:T(8,128)(2,1)S(1)}, bf16[2,3,288,768]{3,2,0,1:T(8,128)(2,1)}, u32[]{:S(2)}) copy-start(bf16[2,3,288,768]{3,2,0,1:T(8,128)(2,1)} %add_convert_fusion) | copy-start | bytes 7962628
  201.1 2.5 copy-start.42
  206.9 35.8 %all-to-all-start.2 = ((bf16[8,96,576]{2,1,0:T(8,128)(2,1)}), bf16[8,96,576]{2,1,0:T(8,128)(2,1)S(1)}, u32[]{:S(2)}, u32[]{:S(2)}) async-start(bf16[8,96,576]{2,1,0:T(8,128)(2,1)} %bitcast.37), calls=%async_computation.3 | async-start | bytes 1966080 | tf_op jit(solution)/shard_map/all_to_all | solution.py:267
  243.5 3.8 %copy-start.24 = (bf16[768,192]{0,1:T(8,128)(2,1)S(1)}, bf16[768,192]{0,1:T(8,128)(2,1)}, u32[]{:S(2)}) copy-start(bf16[768,192]{0,1:T(8,128)(2,1)} %get-tuple-element.81) | copy-start | bytes 884740
  243.5 3.8 %copy-start.26 = (bf16[768,192]{0,1:T(8,128)(2,1)S(1)}, bf16[768,192]{0,1:T(8,128)(2,1)}, u32[]{:S(2)}) copy-start(bf16[768,192]{0,1:T(8,128)(2,1)} %get-tuple-element.82) | copy-start | bytes 884740
  243.5 3.8 %copy-start.28 = (bf16[768,192]{0,1:T(8,128)(2,1)S(1)}, bf16[768,192]{0,1:T(8,128)(2,1)}, u32[]{:S(2)}) copy-start(bf16[768,192]{0,1:T(8,128)(2,1)} %get-tuple-element.84) | copy-start | bytes 884740
  243.5 44.9 %all-to-all-start.3 = ((bf16[8,144,768]{2,1,0:T(8,128)(2,1)}), bf16[8,144,768]{2,1,0:T(8,128)(2,1)S(1)}, u32[]{:S(2)}, u32[]{:S(2)}) async-start(bf16[8,144,768]{2,1,0:T(8,128)(2,1)} %bitcast.130), calls=%async_computation.4 | async-start | bytes 3538944 | tf_op jit(solution)/shard_map/all_to_all | solution.py:267
  247.2 102.0 %all-gather.8.cloned.1.call-start = ((), (), s32[]{:S(2)}) async-start(), calls=%async_computation.8 | async-start | bytes 1990656 | tf_op jit(solution)/shard_map/all_gather | solution.py:272
  251.6 2.1 copy-start.15
  253.0 36.4 %copy-start.9 = (f32[512,768]{1,0:T(8,128)S(1)}, f32[512,768]{1,0:T(8,128)}, u32[]{:S(2)}) copy-start(f32[512,768]{1,0:T(8,128)} %copy-done.8) | copy-start | bytes 4718596
  253.7 39.9 %collective-permute-start.12 = (bf16[512,768]{1,0:T(8,128)(2,1)}, bf16[512,768]{1,0:T(8,128)(2,1)}, u32[]{:S(2)}, u32[]{:S(2)}) collective-permute-start(bf16[512,768]{1,0:T(8,128)(2,1)} %get-tuple-element.73), channel_id=1, source_target_pairs={{0,1},{1,0},{2,3},{3,2},{4,5},{5,4},{6,7},{7,6},{8,9},{9,8},{10,11... | collective-permute-start | bytes 2359304 | tf_op jit(solution)/shard_map/ppermute | solution.py:262
  293.6 3.9 %copy-start.35 = (bf16[96,576]{1,0:T(8,128)(2,1)S(1)}, bf16[96,576]{1,0:T(8,128)(2,1)}, u32[]{:S(2)}) copy-start(bf16[96,576]{1,0:T(8,128)(2,1)} %reduce_sum.143) | copy-start | bytes 331780
  293.6 49.1 %collective-permute-start.11 = (bf16[512,768]{1,0:T(8,128)(2,1)}, bf16[512,768]{1,0:T(8,128)(2,1)S(1)}, u32[]{:S(2)}, u32[]{:S(2)}) collective-permute-start(bf16[512,768]{1,0:T(8,128)(2,1)} %get-tuple-element.72), channel_id=1, source_target_pairs={{0,1},{1,0},{2,3},{3,2},{4,5},{5,4},{6,7},{7,6},{8,9},{9,8},{10,11... | collective-permute-start | bytes 2359304 | tf_op jit(solution)/shard_map/ppermute | solution.py:262
  296.1 46.7 %collective-permute-start.13 = (bf16[512,768]{1,0:T(8,128)(2,1)}, bf16[512,768]{1,0:T(8,128)(2,1)}, u32[]{:S(2)}, u32[]{:S(2)}) collective-permute-start(bf16[512,768]{1,0:T(8,128)(2,1)} %fusion.12), channel_id=1, source_target_pairs={{0,2},{1,3},{2,0},{3,1},{4,6},{5,7},{6,4},{7,5},{8,10},{9,11},{10,... | collective-permute-start | bytes 2359304 | tf_op jit(solution)/shard_map/ppermute | solution.py:262
  341.3 2.5 copy-start.16
  341.4 2.9 copy-start.7
  342.7 3.5 copy-start.12
  351.7 2.1 copy-start.14
  (19 other events, 23.3 us)
Sparse Core Ops, SparseCore 0:
  10.7 31.2 all-gather.3
  51.8 25.1 all-gather.5
  158.0 36.0 reduce-scatter.1
  289.5 52.5 all-gather.7
